TPU v7x, 32 devices: a whole 2x2x4 slice. The times are simulated.
32 devices in a mesh: groups: 2 (over x), wide: 16 (over z, y, core).
Axes of the slice: x: 2, y: 2, z: 4, core: 2. Of those that a mesh axis runs over, the one named last changes fastest.
Arguments:
- queries: bfloat16 [4096, 4096], P(('groups', 'wide')), parts along dimension 0, may hold values from -64 to 64
- first_keys: bfloat16 [4096, 4096], P(('groups', 'wide')), parts along dimension 0, may hold values from -4 to 4
- first_values: bfloat16 [4096, 4096], P(('groups', 'wide')), parts along dimension 0, may hold values from -6 to 6
- second_keys: bfloat16 [4096, 4096], P(('groups', 'wide')), parts along dimension 0, may hold values from -4 to 4
- second_values: bfloat16 [4096, 4096], P(('groups', 'wide')), parts along dimension 0, may hold values from -6 to 6
- out_weight: bfloat16 [4096, 2048], P('wide'), may hold values from -0.09375 to 0.09375
- norm_gain: float32 [2048], replicated, may hold values from 0.1 to 1.9
- gate_weight: bfloat16 [32, 2048, 768], P('wide'), may hold values from -0.125 to 0.125
- up_weight: bfloat16 [32, 2048, 768], P('wide'), may hold values from -0.125 to 0.125
- down_weight: bfloat16 [32, 768, 2048], P('wide'), may hold values from -0.21875 to 0.21875
- routes: int32 [4096, 4], P(('groups', 'wide')), parts along dimension 0, may hold values from 0 to 255, as said below
- route_weights: float32 [4096, 4], P(('groups', 'wide')), parts along dimension 0, may hold values from 0.2 to 1
Outputs:
- layer_out: bfloat16 [4096, 2048], P(('groups', 'wide')), parts along dimension 0
There are 2 independent parts, one for each index of `groups`. A program takes and returns all parts, laid end to end along the dimension named above; an argument that names none is the same for every part. Nothing has to cross between parts.
Inputs may be any that keep to these rules, and one draw needn't show every extreme that they name: `routes`: each token names four different experts. Every expert is named by exactly 32 tokens of the sequence, and by at most 4 tokens among the rows of one device; each expert is named exactly 4 times by the rows of some device.
All inputs are finite; a program needn't handle non-finite values.
Results may differ from a plain program's by a relative error of at most 0.03.
Values may be sent and summed in bfloat16 or wider, within the bound.
A program may use at most 192 MiB of HBM per device.

v0:
```python
import math

import jax
import jax.numpy as jnp
from jax import lax
from jax.sharding import PartitionSpec as P

HEAD_DIM = 128
WIN_KEYS = 512
WIN_PAIRS = 12
CAP = 4


def shifted(x, axis, by):
    devices = lax.axis_size(axis)
    pairs = [(i, i + by) for i in range(devices) if 0 <= i + by < devices]
    return lax.ppermute(x, axis, pairs)


def split_heads(matrix, groups, per_step):
    return matrix.reshape(matrix.shape[0], groups, per_step, HEAD_DIM).transpose(1, 0, 2, 3)


def window_stack(extended, length):
    return jnp.stack(
        [
            extended[WIN_PAIRS - 1 - offset : WIN_PAIRS - 1 - offset + length]
            for offset in range(WIN_PAIRS)
        ],
        axis=1,
    )


def group_attention(pieces, query_start, key_start):
    query_rows, keys_window, values_window, pair_keys_ext, pair_values_ext = pieces
    length = query_rows.shape[0]
    pair_keys = window_stack(pair_keys_ext, length)
    pair_values = window_stack(pair_values_ext, length)
    pair_query = query_rows[:, None] * pair_keys
    scores = jnp.einsum(
        "trgd,lgd->tgrl", pair_query, keys_window, preferred_element_type=jnp.float32
    ) * (1.0 / math.sqrt(HEAD_DIM))
    query_pos = query_start + jnp.arange(length, dtype=jnp.int32)
    key_pos = key_start + jnp.arange(keys_window.shape[0], dtype=jnp.int32)
    offsets = jnp.arange(WIN_PAIRS, dtype=jnp.int32)
    near_mask = (
        (key_pos[None, :] <= query_pos[:, None])
        & (key_pos[None, :] > query_pos[:, None] - WIN_KEYS)
        & (key_pos[None, :] >= 0)
    )
    pair_mask = query_pos[:, None] - offsets[None, :] >= 0
    allowed = near_mask[:, None, None, :] & pair_mask[:, None, :, None]
    scores = jnp.where(allowed, scores, -jnp.inf)
    row_top = jnp.max(scores, axis=(2, 3), keepdims=True)
    raised = jnp.exp(scores - row_top)
    weights = (raised / jnp.sum(raised, axis=(2, 3), keepdims=True)).astype(jnp.bfloat16)
    partial_value = jnp.einsum(
        "tgrl,lgd->tgrd", weights, values_window, preferred_element_type=jnp.float32
    )
    combined = jnp.sum(
        partial_value * pair_values.transpose(0, 2, 1, 3).astype(jnp.float32), axis=2
    )
    return combined.astype(jnp.bfloat16)


def on_device(
    queries,
    first_keys,
    first_values,
    second_keys,
    second_values,
    out_weight,
    norm_gain,
    gate_weight,
    up_weight,
    down_weight,
    routes,
    route_weights,
):
    length = queries.shape[0]
    feature_width = queries.shape[1]
    head_count = feature_width // HEAD_DIM
    per_step = math.gcd(head_count, 4)
    groups = head_count // per_step
    reach_blocks = (WIN_KEYS + length - 2) // length
    device = lax.axis_index("wide")
    devices = lax.axis_size("wide")

    def relay_step(counter, carry):
        moving_keys, moving_values, keys_buffer, values_buffer = carry
        moving_keys, moving_values = shifted((moving_keys, moving_values), "wide", 1)
        place_row = (reach_blocks - 1 - counter) * length
        keys_buffer = lax.dynamic_update_slice_in_dim(keys_buffer, moving_keys, place_row, 0)
        values_buffer = lax.dynamic_update_slice_in_dim(values_buffer, moving_values, place_row, 0)
        return (moving_keys, moving_values, keys_buffer, values_buffer)

    empty_rows = jnp.zeros((reach_blocks * length, feature_width), first_keys.dtype)
    carried = lax.fori_loop(
        0, reach_blocks, relay_step, (first_keys, first_values, empty_rows, empty_rows)
    )
    keys_window = jnp.concatenate([carried[2], first_keys], axis=0)
    values_window = jnp.concatenate([carried[3], first_values], axis=0)
    tail_rows = WIN_PAIRS - 1
    earlier_keys, earlier_values = shifted(
        (second_keys[length - tail_rows :], second_values[length - tail_rows :]), "wide", 1
    )
    pair_keys_ext = jnp.concatenate([earlier_keys, second_keys], axis=0)
    pair_values_ext = jnp.concatenate([earlier_values, second_values], axis=0)
    query_start = device * length
    key_start = query_start - reach_blocks * length
    pieces = tuple(
        (
            split_heads(matrix, groups, per_step)
            for matrix in (queries, keys_window, values_window, pair_keys_ext, pair_values_ext)
        )
    )
    grouped = lax.map(
        lambda group_pieces: group_attention(group_pieces, query_start, key_start), pieces
    )
    attended = grouped.transpose(1, 0, 2, 3).reshape(length, feature_width)
    model_width = out_weight.shape[1]
    projected32 = jnp.dot(
        attended,
        lax.all_gather(out_weight, "wide", axis=0, tiled=True),
        preferred_element_type=jnp.float32,
    )
    projected = projected32.astype(jnp.bfloat16)
    wide_proj = projected.astype(jnp.float32)
    normed = (
        wide_proj
        * lax.rsqrt(jnp.mean(wide_proj * wide_proj, axis=1, keepdims=True) + 1e-06)
        * norm_gain
    ).astype(jnp.bfloat16)
    local_experts = gate_weight.shape[0]
    flight = local_experts * devices
    slot_count = flight * CAP
    route_count = routes.shape[1]
    flat_routes = routes.reshape(-1)
    expert_hits = (flat_routes[:, None] == jnp.arange(flight, dtype=jnp.int32)[None, :]).astype(
        jnp.int32
    )
    earlier = jnp.cumsum(expert_hits, axis=0) - expert_hits
    ranking = jnp.sum(earlier * expert_hits, axis=1)
    in_flight = flat_routes < flight
    target = jnp.where(in_flight, flat_routes * CAP + ranking, slot_count)
    chooser = target[None, :] == jnp.arange(slot_count, dtype=jnp.int32)[:, None]
    token_chooser = jnp.any(chooser.reshape(slot_count, length, route_count), axis=2)
    outgoing = jnp.dot(
        token_chooser.astype(jnp.bfloat16), normed, preferred_element_type=jnp.float32
    ).astype(jnp.bfloat16)
    outgoing = outgoing.reshape(devices, local_experts, CAP, model_width)
    arrived = lax.all_to_all(outgoing, "wide", split_axis=0, concat_axis=0, tiled=True)
    sources, experts_here, kept_slots, row_width = arrived.shape
    expert_rows = arrived.transpose(1, 0, 2, 3).reshape(
        experts_here, sources * kept_slots, row_width
    )
    gate_proj = jnp.einsum(
        "erd,edf->erf", expert_rows, gate_weight, preferred_element_type=jnp.float32
    )
    upward = jnp.einsum("erd,edf->erf", expert_rows, up_weight, preferred_element_type=jnp.float32)
    hidden = (jax.nn.silu(gate_proj) * upward).astype(jnp.bfloat16)
    result = jnp.einsum(
        "erf,efd->erd", hidden, down_weight, preferred_element_type=jnp.float32
    ).astype(jnp.bfloat16)
    finished = result.reshape(experts_here, sources, kept_slots, row_width).transpose(1, 0, 2, 3)
    returned = lax.all_to_all(finished, "wide", split_axis=0, concat_axis=0, tiled=True).reshape(
        slot_count, model_width
    )
    picked = jnp.take(returned, jnp.minimum(target, slot_count - 1), axis=0).astype(jnp.float32)
    route_scale = jnp.where(in_flight, route_weights.reshape(-1), jnp.float32(0.0))
    expert_sum = jnp.sum(
        (picked * route_scale[:, None]).reshape(length, route_count, model_width), axis=1
    )
    return (wide_proj + expert_sum).astype(jnp.bfloat16)


def solution(mesh):
    in_specs = (
        P(("groups", "wide"), None),
        P(("groups", "wide"), None),
        P(("groups", "wide"), None),
        P(("groups", "wide"), None),
        P(("groups", "wide"), None),
        P("wide", None),
        P(),
        P("wide", None, None),
        P("wide", None, None),
        P("wide", None, None),
        P(("groups", "wide"), None),
        P(("groups", "wide"), None),
    )
    out_specs = P(("groups", "wide"), None)
    return jax.shard_map(
        on_device, mesh=mesh, in_specs=in_specs, out_specs=out_specs, check_vma=False
    )
```

profile of v0, /device:TPU:0, one launch (start us, length us, event | category | flops | bytes accessed | tf_op | source)
XLA Modules:
  0.0 706.8 jit_solution(13737942677639050982)
XLA Ops:
  9.4 3.1 collective-permute-start.3
  14.1 3.9 collective-permute-start.2
  23.0 2.6 broadcast_in_dim.66
  27.8 167.2 %while.31 = (s32[]{:T(128)}, bf16[128,4096]{1,0:T(8,128)(2,1)S(1)}, bf16[128,4096]{1,0:T(8,128)(2,1)}, bf16[512,4096]{0,1:T(8,128)(2,1)}, bf16[512,4096]{1,0:T(8...) while((s32[]{:T(128)}, bf16[128,4096]{1,0:T(8,128)(2,1)S(1)}, ...), condition=%wide.region_1.0_spmd, body=%wide.region_0.0_spmd.sunk | while | flops 7 | bytes 23068944 | solution.py:98
  29.8 3.5 collective-permute-start.1
  38.4 27.0 %collective-permute-start = (bf16[128,4096]{1,0:T(8,128)(2,1)S(1)}, bf16[128,4096]{1,0:T(8,128)(2,1)S(1)}, u32[]{:S(2)}, u32[]{:S(2)}) collective-permute-start(bf16[128,4096]{1,0:T(8,128)(2,1)S(1)} %get-tuple-element.430), channel_id=1, source_target_pairs={{0,1},{1,2},{2,3},{3,4},{4,5},{5,6},{6,7},{7,8},{8,9},{9,10},{10,1... | collective-permute-start | bytes 3145736 | tf_op jit(solution)/shard_map/while/body/eval_jaxpr/ppermute | solution.py:17
  65.4 4.3 collective-permute-start.1
  74.6 58.6 %collective-permute-start = (bf16[128,4096]{1,0:T(8,128)(2,1)S(1)}, bf16[128,4096]{1,0:T(8,128)(2,1)S(1)}, u32[]{:S(2)}, u32[]{:S(2)}) collective-permute-start(bf16[128,4096]{1,0:T(8,128)(2,1)S(1)} %get-tuple-element.430), channel_id=1, source_target_pairs={{0,1},{1,2},{2,3},{3,4},{4,5},{5,6},{6,7},{7,8},{8,9},{9,10},{10,1... | collective-permute-start | bytes 3145736 | tf_op jit(solution)/shard_map/while/body/eval_jaxpr/ppermute | solution.py:17
  133.1 4.3 collective-permute-start.1
  142.3 43.6 %collective-permute-start = (bf16[128,4096]{1,0:T(8,128)(2,1)S(1)}, bf16[128,4096]{1,0:T(8,128)(2,1)S(1)}, u32[]{:S(2)}, u32[]{:S(2)}) collective-permute-start(bf16[128,4096]{1,0:T(8,128)(2,1)S(1)} %get-tuple-element.430), channel_id=1, source_target_pairs={{0,1},{1,2},{2,3},{3,4},{4,5},{5,6},{6,7},{7,8},{8,9},{9,10},{10,1... | collective-permute-start | bytes 3145736 | tf_op jit(solution)/shard_map/while/body/eval_jaxpr/ppermute | solution.py:17
  185.9 4.3 collective-permute-start.1
  195.0 5.5 pad_maximum_fusion
  200.5 8.0 %copy.135 = bf16[640,4096]{0,1:T(8,128)(2,1)} copy(bf16[640,4096]{1,0:T(8,128)(2,1)} %pad_maximum_fusion) | data formatting | bytes 10485760 | tf_op jit(solution)/shard_map/concatenate | solution.py:102
  209.7 4.9 pad_maximum_fusion.1
  220.1 363.0 %while.32 = (s32[]{:T(128)}, bf16[8,128,4,128]{1,3,2,0:T(8,128)(2,1)}, bf16[8,640,4,128]{1,3,2,0:T(8,128)(2,1)}, s32[]{:T(128)}, s32[]{:T(128)}, /*index=5*/bf16...) while((s32[]{:T(128)}, ...), condition=%wide.region_6.7_spmd, body=%wide.region_2.6_spmd.sunk | while | flops 2064846976 | bytes 72539904 | solution.py:117
  223.7 10.6 %fusion.116 = (f32[128,4]{0,1:T(4,128)S(1)}, f32[4,640,128,12]{2,1,3,0:T(8,128)}) fusion(pred[128,12,640]{0,2,1:T(8,128)(4,1)S(1)} %broadcast_and_fusion.2, bf16[8,640,4,128]{1,3,2,0:T(8,128)(2,1)} %get-tuple-element.498, s32[]{:T(128)} %get-tuple-element.471, bf16[128,12,4,128]{3,0,2,1:T(8,128)(2,1)} %copy-done.5, bf16[128,4,128]{2,0,1:T(8,128)(2,1)S(1)} %bitcast.272), kind=kOutput, calls=%fused_computation.7.clone.1 | convolution fusion | flops 1019215360 | bytes 19073536 | tf_op jit(solution)/shard_map/while/body/eval_jaxpr/trgd,lgd->tgrl/dot_general | solution.py:40
  234.4 8.8 %fusion.117 = f32[128,4]{0,1:T(4,128)S(1)} fusion(f32[4,640,128,12]{2,1,3,0:T(8,128)} %get-tuple-element.417, f32[128,4]{0,1:T(4,128)S(1)} %get-tuple-element.418, pred[128,12,640]{0,2,1:T(8,128)(4,1)S(1)} %broadcast_and_fusion.2), kind=kLoop, calls=%fused_computation.6.clone.1 | loop fusion | flops 15728128 | bytes 16715776 | tf_op jit(solution)/shard_map/while/body/eval_jaxpr/reduce_sum | solution.py:56
  256.1 8.9 %fusion.118 = bf16[128,4,128]{0,2,1:T(8,128)(2,1)S(1)} fusion(bf16[128,12,4,128]{0,3,1,2:T(8,128)(2,1)S(1)} %fusion.103, f32[4,640,128,12]{2,1,3,0:T(8,128)} %get-tuple-element.417, f32[128,4]{0,1:T(4,128)S(1)} %fusion.117, f32[128,4]{0,1:T(4,128)S(1)} %get-tuple-element.418, pred[128,12,640]{0,2,1:T(8,128)(4,1)S(1)} %broadcast_and_fusion.2, ...), kind=kOutput, calls=%fused_computation.10.clone.1 | convolution fusion | flops 1028587520 | bytes 19075584 | tf_op jit(solution)/shard_map/while/body/eval_jaxpr/tgrl,lgd->tgrd/dot_general | solution.py:57
  269.1 10.6 %fusion.116 = (f32[128,4]{0,1:T(4,128)S(1)}, f32[4,640,128,12]{2,1,3,0:T(8,128)}) fusion(pred[128,12,640]{0,2,1:T(8,128)(4,1)S(1)} %broadcast_and_fusion.2, bf16[8,640,4,128]{1,3,2,0:T(8,128)(2,1)} %get-tuple-element.498, s32[]{:T(128)} %get-tuple-element.471, bf16[128,12,4,128]{3,0,2,1:T(8,128)(2,1)} %copy-done.5, bf16[128,4,128]{2,0,1:T(8,128)(2,1)S(1)} %bitcast.272), kind=kOutput, calls=%fused_computation.7.clone.1 | convolution fusion | flops 1019215360 | bytes 19073536 | tf_op jit(solution)/shard_map/while/body/eval_jaxpr/trgd,lgd->tgrl/dot_general | solution.py:40
  279.7 8.8 %fusion.117 = f32[128,4]{0,1:T(4,128)S(1)} fusion(f32[4,640,128,12]{2,1,3,0:T(8,128)} %get-tuple-element.417, f32[128,4]{0,1:T(4,128)S(1)} %get-tuple-element.418, pred[128,12,640]{0,2,1:T(8,128)(4,1)S(1)} %broadcast_and_fusion.2), kind=kLoop, calls=%fused_computation.6.clone.1 | loop fusion | flops 15728128 | bytes 16715776 | tf_op jit(solution)/shard_map/while/body/eval_jaxpr/reduce_sum | solution.py:56
  301.5 8.9 %fusion.118 = bf16[128,4,128]{0,2,1:T(8,128)(2,1)S(1)} fusion(bf16[128,12,4,128]{0,3,1,2:T(8,128)(2,1)S(1)} %fusion.103, f32[4,640,128,12]{2,1,3,0:T(8,128)} %get-tuple-element.417, f32[128,4]{0,1:T(4,128)S(1)} %fusion.117, f32[128,4]{0,1:T(4,128)S(1)} %get-tuple-element.418, pred[128,12,640]{0,2,1:T(8,128)(4,1)S(1)} %broadcast_and_fusion.2, ...), kind=kOutput, calls=%fused_computation.10.clone.1 | convolution fusion | flops 1028587520 | bytes 19075584 | tf_op jit(solution)/shard_map/while/body/eval_jaxpr/tgrl,lgd->tgrd/dot_general | solution.py:57
  314.4 10.6 %fusion.116 = (f32[128,4]{0,1:T(4,128)S(1)}, f32[4,640,128,12]{2,1,3,0:T(8,128)}) fusion(pred[128,12,640]{0,2,1:T(8,128)(4,1)S(1)} %broadcast_and_fusion.2, bf16[8,640,4,128]{1,3,2,0:T(8,128)(2,1)} %get-tuple-element.498, s32[]{:T(128)} %get-tuple-element.471, bf16[128,12,4,128]{3,0,2,1:T(8,128)(2,1)} %copy-done.5, bf16[128,4,128]{2,0,1:T(8,128)(2,1)S(1)} %bitcast.272), kind=kOutput, calls=%fused_computation.7.clone.1 | convolution fusion | flops 1019215360 | bytes 19073536 | tf_op jit(solution)/shard_map/while/body/eval_jaxpr/trgd,lgd->tgrl/dot_general | solution.py:40
  325.1 8.8 %fusion.117 = f32[128,4]{0,1:T(4,128)S(1)} fusion(f32[4,640,128,12]{2,1,3,0:T(8,128)} %get-tuple-element.417, f32[128,4]{0,1:T(4,128)S(1)} %get-tuple-element.418, pred[128,12,640]{0,2,1:T(8,128)(4,1)S(1)} %broadcast_and_fusion.2), kind=kLoop, calls=%fused_computation.6.clone.1 | loop fusion | flops 15728128 | bytes 16715776 | tf_op jit(solution)/shard_map/while/body/eval_jaxpr/reduce_sum | solution.py:56
  346.8 8.9 %fusion.118 = bf16[128,4,128]{0,2,1:T(8,128)(2,1)S(1)} fusion(bf16[128,12,4,128]{0,3,1,2:T(8,128)(2,1)S(1)} %fusion.103, f32[4,640,128,12]{2,1,3,0:T(8,128)} %get-tuple-element.417, f32[128,4]{0,1:T(4,128)S(1)} %fusion.117, f32[128,4]{0,1:T(4,128)S(1)} %get-tuple-element.418, pred[128,12,640]{0,2,1:T(8,128)(4,1)S(1)} %broadcast_and_fusion.2, ...), kind=kOutput, calls=%fused_computation.10.clone.1 | convolution fusion | flops 1028587520 | bytes 19075584 | tf_op jit(solution)/shard_map/while/body/eval_jaxpr/tgrl,lgd->tgrd/dot_general | solution.py:57
  359.8 10.6 %fusion.116 = (f32[128,4]{0,1:T(4,128)S(1)}, f32[4,640,128,12]{2,1,3,0:T(8,128)}) fusion(pred[128,12,640]{0,2,1:T(8,128)(4,1)S(1)} %broadcast_and_fusion.2, bf16[8,640,4,128]{1,3,2,0:T(8,128)(2,1)} %get-tuple-element.498, s32[]{:T(128)} %get-tuple-element.471, bf16[128,12,4,128]{3,0,2,1:T(8,128)(2,1)} %copy-done.5, bf16[128,4,128]{2,0,1:T(8,128)(2,1)S(1)} %bitcast.272), kind=kOutput, calls=%fused_computation.7.clone.1 | convolution fusion | flops 1019215360 | bytes 19073536 | tf_op jit(solution)/shard_map/while/body/eval_jaxpr/trgd,lgd->tgrl/dot_general | solution.py:40
  370.4 8.8 %fusion.117 = f32[128,4]{0,1:T(4,128)S(1)} fusion(f32[4,640,128,12]{2,1,3,0:T(8,128)} %get-tuple-element.417, f32[128,4]{0,1:T(4,128)S(1)} %get-tuple-element.418, pred[128,12,640]{0,2,1:T(8,128)(4,1)S(1)} %broadcast_and_fusion.2), kind=kLoop, calls=%fused_computation.6.clone.1 | loop fusion | flops 15728128 | bytes 16715776 | tf_op jit(solution)/shard_map/while/body/eval_jaxpr/reduce_sum | solution.py:56
  392.2 8.9 %fusion.118 = bf16[128,4,128]{0,2,1:T(8,128)(2,1)S(1)} fusion(bf16[128,12,4,128]{0,3,1,2:T(8,128)(2,1)S(1)} %fusion.103, f32[4,640,128,12]{2,1,3,0:T(8,128)} %get-tuple-element.417, f32[128,4]{0,1:T(4,128)S(1)} %fusion.117, f32[128,4]{0,1:T(4,128)S(1)} %get-tuple-element.418, pred[128,12,640]{0,2,1:T(8,128)(4,1)S(1)} %broadcast_and_fusion.2, ...), kind=kOutput, calls=%fused_computation.10.clone.1 | convolution fusion | flops 1028587520 | bytes 19075584 | tf_op jit(solution)/shard_map/while/body/eval_jaxpr/tgrl,lgd->tgrd/dot_general | solution.py:57
  405.1 10.6 %fusion.116 = (f32[128,4]{0,1:T(4,128)S(1)}, f32[4,640,128,12]{2,1,3,0:T(8,128)}) fusion(pred[128,12,640]{0,2,1:T(8,128)(4,1)S(1)} %broadcast_and_fusion.2, bf16[8,640,4,128]{1,3,2,0:T(8,128)(2,1)} %get-tuple-element.498, s32[]{:T(128)} %get-tuple-element.471, bf16[128,12,4,128]{3,0,2,1:T(8,128)(2,1)} %copy-done.5, bf16[128,4,128]{2,0,1:T(8,128)(2,1)S(1)} %bitcast.272), kind=kOutput, calls=%fused_computation.7.clone.1 | convolution fusion | flops 1019215360 | bytes 19073536 | tf_op jit(solution)/shard_map/while/body/eval_jaxpr/trgd,lgd->tgrl/dot_general | solution.py:40
  415.8 8.8 %fusion.117 = f32[128,4]{0,1:T(4,128)S(1)} fusion(f32[4,640,128,12]{2,1,3,0:T(8,128)} %get-tuple-element.417, f32[128,4]{0,1:T(4,128)S(1)} %get-tuple-element.418, pred[128,12,640]{0,2,1:T(8,128)(4,1)S(1)} %broadcast_and_fusion.2), kind=kLoop, calls=%fused_computation.6.clone.1 | loop fusion | flops 15728128 | bytes 16715776 | tf_op jit(solution)/shard_map/while/body/eval_jaxpr/reduce_sum | solution.py:56
  437.5 8.9 %fusion.118 = bf16[128,4,128]{0,2,1:T(8,128)(2,1)S(1)} fusion(bf16[128,12,4,128]{0,3,1,2:T(8,128)(2,1)S(1)} %fusion.103, f32[4,640,128,12]{2,1,3,0:T(8,128)} %get-tuple-element.417, f32[128,4]{0,1:T(4,128)S(1)} %fusion.117, f32[128,4]{0,1:T(4,128)S(1)} %get-tuple-element.418, pred[128,12,640]{0,2,1:T(8,128)(4,1)S(1)} %broadcast_and_fusion.2, ...), kind=kOutput, calls=%fused_computation.10.clone.1 | convolution fusion | flops 1028587520 | bytes 19075584 | tf_op jit(solution)/shard_map/while/body/eval_jaxpr/tgrl,lgd->tgrd/dot_general | solution.py:57
  450.5 10.6 %fusion.116 = (f32[128,4]{0,1:T(4,128)S(1)}, f32[4,640,128,12]{2,1,3,0:T(8,128)}) fusion(pred[128,12,640]{0,2,1:T(8,128)(4,1)S(1)} %broadcast_and_fusion.2, bf16[8,640,4,128]{1,3,2,0:T(8,128)(2,1)} %get-tuple-element.498, s32[]{:T(128)} %get-tuple-element.471, bf16[128,12,4,128]{3,0,2,1:T(8,128)(2,1)} %copy-done.5, bf16[128,4,128]{2,0,1:T(8,128)(2,1)S(1)} %bitcast.272), kind=kOutput, calls=%fused_computation.7.clone.1 | convolution fusion | flops 1019215360 | bytes 19073536 | tf_op jit(solution)/shard_map/while/body/eval_jaxpr/trgd,lgd->tgrl/dot_general | solution.py:40
  461.1 8.8 %fusion.117 = f32[128,4]{0,1:T(4,128)S(1)} fusion(f32[4,640,128,12]{2,1,3,0:T(8,128)} %get-tuple-element.417, f32[128,4]{0,1:T(4,128)S(1)} %get-tuple-element.418, pred[128,12,640]{0,2,1:T(8,128)(4,1)S(1)} %broadcast_and_fusion.2), kind=kLoop, calls=%fused_computation.6.clone.1 | loop fusion | flops 15728128 | bytes 16715776 | tf_op jit(solution)/shard_map/while/body/eval_jaxpr/reduce_sum | solution.py:56
  482.8 8.9 %fusion.118 = bf16[128,4,128]{0,2,1:T(8,128)(2,1)S(1)} fusion(bf16[128,12,4,128]{0,3,1,2:T(8,128)(2,1)S(1)} %fusion.103, f32[4,640,128,12]{2,1,3,0:T(8,128)} %get-tuple-element.417, f32[128,4]{0,1:T(4,128)S(1)} %fusion.117, f32[128,4]{0,1:T(4,128)S(1)} %get-tuple-element.418, pred[128,12,640]{0,2,1:T(8,128)(4,1)S(1)} %broadcast_and_fusion.2, ...), kind=kOutput, calls=%fused_computation.10.clone.1 | convolution fusion | flops 1028587520 | bytes 19075584 | tf_op jit(solution)/shard_map/while/body/eval_jaxpr/tgrl,lgd->tgrd/dot_general | solution.py:57
  495.8 10.6 %fusion.116 = (f32[128,4]{0,1:T(4,128)S(1)}, f32[4,640,128,12]{2,1,3,0:T(8,128)}) fusion(pred[128,12,640]{0,2,1:T(8,128)(4,1)S(1)} %broadcast_and_fusion.2, bf16[8,640,4,128]{1,3,2,0:T(8,128)(2,1)} %get-tuple-element.498, s32[]{:T(128)} %get-tuple-element.471, bf16[128,12,4,128]{3,0,2,1:T(8,128)(2,1)} %copy-done.5, bf16[128,4,128]{2,0,1:T(8,128)(2,1)S(1)} %bitcast.272), kind=kOutput, calls=%fused_computation.7.clone.1 | convolution fusion | flops 1019215360 | bytes 19073536 | tf_op jit(solution)/shard_map/while/body/eval_jaxpr/trgd,lgd->tgrl/dot_general | solution.py:40
  506.4 8.8 %fusion.117 = f32[128,4]{0,1:T(4,128)S(1)} fusion(f32[4,640,128,12]{2,1,3,0:T(8,128)} %get-tuple-element.417, f32[128,4]{0,1:T(4,128)S(1)} %get-tuple-element.418, pred[128,12,640]{0,2,1:T(8,128)(4,1)S(1)} %broadcast_and_fusion.2), kind=kLoop, calls=%fused_computation.6.clone.1 | loop fusion | flops 15728128 | bytes 16715776 | tf_op jit(solution)/shard_map/while/body/eval_jaxpr/reduce_sum | solution.py:56
  528.2 8.9 %fusion.118 = bf16[128,4,128]{0,2,1:T(8,128)(2,1)S(1)} fusion(bf16[128,12,4,128]{0,3,1,2:T(8,128)(2,1)S(1)} %fusion.103, f32[4,640,128,12]{2,1,3,0:T(8,128)} %get-tuple-element.417, f32[128,4]{0,1:T(4,128)S(1)} %fusion.117, f32[128,4]{0,1:T(4,128)S(1)} %get-tuple-element.418, pred[128,12,640]{0,2,1:T(8,128)(4,1)S(1)} %broadcast_and_fusion.2, ...), kind=kOutput, calls=%fused_computation.10.clone.1 | convolution fusion | flops 1028587520 | bytes 19075584 | tf_op jit(solution)/shard_map/while/body/eval_jaxpr/tgrl,lgd->tgrd/dot_general | solution.py:57
  541.2 10.6 %fusion.116 = (f32[128,4]{0,1:T(4,128)S(1)}, f32[4,640,128,12]{2,1,3,0:T(8,128)}) fusion(pred[128,12,640]{0,2,1:T(8,128)(4,1)S(1)} %broadcast_and_fusion.2, bf16[8,640,4,128]{1,3,2,0:T(8,128)(2,1)} %get-tuple-element.498, s32[]{:T(128)} %get-tuple-element.471, bf16[128,12,4,128]{3,0,2,1:T(8,128)(2,1)} %copy-done.5, bf16[128,4,128]{2,0,1:T(8,128)(2,1)S(1)} %bitcast.272), kind=kOutput, calls=%fused_computation.7.clone.1 | convolution fusion | flops 1019215360 | bytes 19073536 | tf_op jit(solution)/shard_map/while/body/eval_jaxpr/trgd,lgd->tgrl/dot_general | solution.py:40
  551.8 8.8 %fusion.117 = f32[128,4]{0,1:T(4,128)S(1)} fusion(f32[4,640,128,12]{2,1,3,0:T(8,128)} %get-tuple-element.417, f32[128,4]{0,1:T(4,128)S(1)} %get-tuple-element.418, pred[128,12,640]{0,2,1:T(8,128)(4,1)S(1)} %broadcast_and_fusion.2), kind=kLoop, calls=%fused_computation.6.clone.1 | loop fusion | flops 15728128 | bytes 16715776 | tf_op jit(solution)/shard_map/while/body/eval_jaxpr/reduce_sum | solution.py:56
  573.6 8.9 %fusion.118 = bf16[128,4,128]{0,2,1:T(8,128)(2,1)S(1)} fusion(bf16[128,12,4,128]{0,3,1,2:T(8,128)(2,1)S(1)} %fusion.103, f32[4,640,128,12]{2,1,3,0:T(8,128)} %get-tuple-element.417, f32[128,4]{0,1:T(4,128)S(1)} %fusion.117, f32[128,4]{0,1:T(4,128)S(1)} %get-tuple-element.418, pred[128,12,640]{0,2,1:T(8,128)(4,1)S(1)} %broadcast_and_fusion.2, ...), kind=kOutput, calls=%fused_computation.10.clone.1 | convolution fusion | flops 1028587520 | bytes 19075584 | tf_op jit(solution)/shard_map/while/body/eval_jaxpr/tgrl,lgd->tgrd/dot_general | solution.py:57
  583.1 8.6 %multiply_reduce_fusion.1 = (f32[128]{0:T(128)S(1)}, f32[128,2048]{1,0:T(8,128)S(1)}) fusion(bf16[128,4096]{0,1:T(8,128)(2,1)} %bitcast.56, bf16[4096,2048]{1,0:T(8,128)(2,1)} %all-gather.2.cloned.1.call-done), kind=kOutput, calls=%fused_computation.104 | convolution fusion | flops 2148532224 | bytes 18874880 | tf_op jit(solution)/shard_map/dot_general | solution.py:122
  592.3 62.6 %all_to_all.10 = bf16[16,2,4,2048]{3,2,1,0:T(4,128)(2,1)S(1)} all-to-all(bf16[16,2,4,2048]{3,2,1,0:T(4,128)(2,1)S(1)} %reshape.332), channel_id=1, replica_groups=mesh['groups'=2,'wide'=16] {'wide'}, dimensions={0} | all-to-all | bytes 1048576 | tf_op jit(solution)/shard_map/all_to_all | solution.py:152
  655.3 3.9 fusion.54
  659.2 6.9 convolution_convert_fusion
  667.3 4.1 all-to-all-start.1
  672.2 13.6 %all-to-all-done.1 = bf16[16,2,4,2048]{3,2,1,0:T(4,128)(2,1)S(1)} async-done(((bf16[16,2,4,2048]{3,2,1,0:T(4,128)(2,1)}), bf16[16,2,4,2048]{3,2,1,0:T(4,128)(2,1)S(1)}, u32[]{:S(2)}, u32[]{:S(2)}) %all-to-all-start.1) | async-done | bytes 524320 | tf_op jit(solution)/shard_map/all_to_all | solution.py:166
  686.0 3.3 gather_fusion
  689.3 4.1 gather.7
  693.4 5.6 multiply_reduce_fusion
  (400 shorter events, 178.4 us)
Async XLA Ops:
  6.5 11.5 %copy-start.7 = (s32[128,4]{0,1:T(4,128)S(1)}, s32[128,4]{0,1:T(4,128)}, u32[]{:S(2)}) copy-start(s32[128,4]{0,1:T(4,128)} %param.26) | copy-start | bytes 6148
  6.5 576.6 %all-gather.2.cloned.1.call-start = ((), (), s32[]{:S(2)}) async-start(), calls=%async_computation.2 | async-start | bytes 17825792 | tf_op jit(solution)/shard_map/all_gather | solution.py:124
  9.4 12.6 %copy-start = (bf16[128,4096]{1,0:T(8,128)(2,1)S(1)}, bf16[128,4096]{1,0:T(8,128)(2,1)}, u32[]{:S(2)}) copy-start(bf16[128,4096]{1,0:T(8,128)(2,1)} %param.18) | copy-start | bytes 3145732
  9.4 205.9 %collective-permute-start.3 = (bf16[11,4096]{1,0:T(8,128)(2,1)}, bf16[11,4096]{1,0:T(8,128)(2,1)}, u32[]{:S(2)}, u32[]{:S(2)}) collective-permute-start(bf16[11,4096]{1,0:T(8,128)(2,1)} %slice.181), channel_id=1, source_target_pairs={{0,1},{1,2},{2,3},{3,4},{4,5},{5,6},{6,7},{7,8},{8,9},{9,10},{10,1... | collective-permute-start | bytes 270344 | tf_op jit(solution)/shard_map/ppermute | solution.py:17
  14.1 205.1 %collective-permute-start.2 = (bf16[11,4096]{1,0:T(8,128)(2,1)}, bf16[11,4096]{1,0:T(8,128)(2,1)S(1)}, u32[]{:S(2)}, u32[]{:S(2)}) collective-permute-start(bf16[11,4096]{1,0:T(8,128)(2,1)} %slice.180), channel_id=1, source_target_pairs={{0,1},{1,2},{2,3},{3,4},{4,5},{5,6},{6,7},{7,8},{8,9},{9,10},{10,1... | collective-permute-start | bytes 270344 | tf_op jit(solution)/shard_map/ppermute | solution.py:17
  21.2 4.3 copy-start.9
  27.8 5.5 collective-permute-start
  29.8 6.5 collective-permute-start.1
  36.3 2.1 copy-start.2
  38.4 31.3 %collective-permute-start = (bf16[128,4096]{1,0:T(8,128)(2,1)S(1)}, bf16[128,4096]{1,0:T(8,128)(2,1)S(1)}, u32[]{:S(2)}, u32[]{:S(2)}) collective-permute-start(bf16[128,4096]{1,0:T(8,128)(2,1)S(1)} %get-tuple-element.430), channel_id=1, source_target_pairs={{0,1},{1,2},{2,3},{3,4},{4,5},{5,6},{6,7},{7,8},{8,9},{9,10},{10,1... | collective-permute-start | bytes 3145736 | tf_op jit(solution)/shard_map/while/body/eval_jaxpr/ppermute | solution.py:17
  65.4 7.1 %collective-permute-start.1 = (bf16[128,4096]{1,0:T(8,128)(2,1)}, bf16[128,4096]{1,0:T(8,128)(2,1)S(1)}, u32[]{:S(2)}, u32[]{:S(2)}) collective-permute-start(bf16[128,4096]{1,0:T(8,128)(2,1)} %get-tuple-element.431), channel_id=1, source_target_pairs={{0,1},{1,2},{2,3},{3,4},{4,5},{5,6},{6,7},{7,8},{8,9},{9,10},{10,1... | collective-permute-start | bytes 3145736 | tf_op jit(solution)/shard_map/while/body/eval_jaxpr/ppermute | solution.py:17
  72.5 2.0 copy-start.2
  74.6 62.9 %collective-permute-start = (bf16[128,4096]{1,0:T(8,128)(2,1)S(1)}, bf16[128,4096]{1,0:T(8,128)(2,1)S(1)}, u32[]{:S(2)}, u32[]{:S(2)}) collective-permute-start(bf16[128,4096]{1,0:T(8,128)(2,1)S(1)} %get-tuple-element.430), channel_id=1, source_target_pairs={{0,1},{1,2},{2,3},{3,4},{4,5},{5,6},{6,7},{7,8},{8,9},{9,10},{10,1... | collective-permute-start | bytes 3145736 | tf_op jit(solution)/shard_map/while/body/eval_jaxpr/ppermute | solution.py:17
  133.1 7.1 %collective-permute-start.1 = (bf16[128,4096]{1,0:T(8,128)(2,1)}, bf16[128,4096]{1,0:T(8,128)(2,1)S(1)}, u32[]{:S(2)}, u32[]{:S(2)}) collective-permute-start(bf16[128,4096]{1,0:T(8,128)(2,1)} %get-tuple-element.431), channel_id=1, source_target_pairs={{0,1},{1,2},{2,3},{3,4},{4,5},{5,6},{6,7},{7,8},{8,9},{9,10},{10,1... | collective-permute-start | bytes 3145736 | tf_op jit(solution)/shard_map/while/body/eval_jaxpr/ppermute | solution.py:17
  140.3 2.0 copy-start.2
  142.3 47.9 %collective-permute-start = (bf16[128,4096]{1,0:T(8,128)(2,1)S(1)}, bf16[128,4096]{1,0:T(8,128)(2,1)S(1)}, u32[]{:S(2)}, u32[]{:S(2)}) collective-permute-start(bf16[128,4096]{1,0:T(8,128)(2,1)S(1)} %get-tuple-element.430), channel_id=1, source_target_pairs={{0,1},{1,2},{2,3},{3,4},{4,5},{5,6},{6,7},{7,8},{8,9},{9,10},{10,1... | collective-permute-start | bytes 3145736 | tf_op jit(solution)/shard_map/while/body/eval_jaxpr/ppermute | solution.py:17
  185.9 7.1 %collective-permute-start.1 = (bf16[128,4096]{1,0:T(8,128)(2,1)}, bf16[128,4096]{1,0:T(8,128)(2,1)S(1)}, u32[]{:S(2)}, u32[]{:S(2)}) collective-permute-start(bf16[128,4096]{1,0:T(8,128)(2,1)} %get-tuple-element.431), channel_id=1, source_target_pairs={{0,1},{1,2},{2,3},{3,4},{4,5},{5,6},{6,7},{7,8},{8,9},{9,10},{10,1... | collective-permute-start | bytes 3145736 | tf_op jit(solution)/shard_map/while/body/eval_jaxpr/ppermute | solution.py:17
  193.0 2.0 copy-start.2
  200.5 8.0 %copy-start.4 = (bf16[128,4096]{1,0:T(8,128)(2,1)S(1)}, bf16[128,4096]{1,0:T(8,128)(2,1)}, u32[]{:S(2)}) copy-start(bf16[128,4096]{1,0:T(8,128)(2,1)} %param.16) | copy-start | bytes 3145732
  208.5 1.2 copy-start.1
  216.8 2.5 copy-start.3
  221.6 1.1 copy-start.5
  267.0 1.1 copy-start.5
  312.3 1.1 copy-start.5
  357.7 1.1 copy-start.5
  403.0 1.1 copy-start.5
  448.4 1.1 copy-start.5
  493.7 1.1 copy-start.5
  539.1 1.1 copy-start.5
  583.1 8.6 %copy-start.6 = (pred[128,128]{1,0:T(8,128)(4,1)S(1)}, pred[128,128]{1,0:T(8,128)(4,1)}, u32[]{:S(2)}) copy-start(pred[128,128]{1,0:T(8,128)(4,1)} %fusion.47) | copy-start | bytes 49156
  583.1 8.6 %copy-start.11 = (f32[2048]{0:T(1024)S(1)}, f32[2048]{0:T(1024)}, u32[]{:S(2)}) copy-start(f32[2048]{0:T(1024)} %param.22) | copy-start | bytes 24580
  666.0 5.4 copy-start.12
  666.0 5.6 copy-start.8
  666.1 5.9 copy-start.14
  666.1 6.0 copy-start.13
  666.1 6.1 copy-start.10
  667.3 18.6 %all-to-all-start.1 = ((bf16[16,2,4,2048]{3,2,1,0:T(4,128)(2,1)}), bf16[16,2,4,2048]{3,2,1,0:T(4,128)(2,1)S(1)}, u32[]{:S(2)}, u32[]{:S(2)}) async-start(bf16[16,2,4,2048]{3,2,1,0:T(4,128)(2,1)} %bitcast.201), calls=%async_computation.1 | async-start | bytes 1048576 | tf_op jit(solution)/shard_map/all_to_all | solution.py:166
Sparse Core Ops, SparseCore 0:
  18.1 156.2 all-gather.1
where the time goes:
time: 711 us; the launch traced here: 707 us
  local copies, waits for them, and re-layouts  183 us (26%)
  matrix products  176 us (25%)
  starting transfers between devices  159 us (22%)
  other arithmetic  98.1 us (14%)
  blocking collectives  62.6 us (9%)
  waiting for transfers between devices  13.7 us (2%)
  between operations  13.7 us (2%)
    ppermute x10, starting transfers between devices, shifted(): return lax.ppermute(x, axis, pairs)  154 us
    while x208, local copies, waits for them, and re-layouts  116 us
    dot_general x8, matrix products, group_attention(): jnp.einsum('trgd,lgd->tgrl', pair_query, keys_window, preferred_element_t...  85 us
    dot_general x8, matrix products, group_attention(): jnp.einsum('tgrl,lgd->tgrd', weights, values_window, preferred_element_ty...  71 us
    reduce_sum x8, other arithmetic, group_attention(): jnp.sum(raised, axis=(2, 3), keepdims=True)  70.6 us
    all_to_all x1, blocking collectives, on_device(): lax.all_to_all(outgoing, 'wide', split_axis=0, concat_axis=0, tiled=True)  62.6 us
  transfers between devices with their start and end apart: 12, of which 1 were waited for; matrix products, arithmetic and copies ran while one was open for 58% of the time, Pallas kernels for 0%

commit v1 on v0

v1 whole, which is shorter than its diff:
```python
import functools
import math

import jax
import jax.numpy as jnp
from jax import lax
from jax.experimental import pallas as pl
from jax.experimental.pallas import tpu as pltpu
from jax.sharding import PartitionSpec as P

HEAD_DIM = 128
WIN_KEYS = 512
WIN_PAIRS = 12
CAP = 4
TAIL = 16
FAR = -1e30
SCALE = math.log2(math.e) / math.sqrt(HEAD_DIM)


def head_columns(head):
    return pl.ds(pl.multiple_of(head * HEAD_DIM, HEAD_DIM), HEAD_DIM)


def build_masks(device, length, blocks, keys_ext, pair_query, values_ext, alive):
    row = lax.broadcasted_iota(jnp.int32, (length, length), 0)
    col = lax.broadcasted_iota(jnp.int32, (length, length), 1)
    odd = lax.rem(device, 2)
    distances = (blocks - 1, 2, jnp.where(odd == 1, 1, 3), jnp.where(odd == 1, 3, 1), 0)
    for place, distance in enumerate(distances):
        if place == 0:
            admitted = row > col
        elif place == blocks - 1:
            admitted = row <= col
        else:
            admitted = row >= 0
        admitted = admitted & (device >= distance)
        keys_ext[place * length:(place + 1) * length, HEAD_DIM:] = jnp.where(
            admitted, 0.0, FAR
        ).astype(jnp.bfloat16)
    identity = jnp.where(row == col, 1.0, 0.0).astype(jnp.bfloat16)
    for offset in range(WIN_PAIRS):
        pair_query[offset * length:(offset + 1) * length, HEAD_DIM:] = identity
    values_ext[:, HEAD_DIM:] = jnp.ones((blocks * length, HEAD_DIM), jnp.bfloat16)
    ext_row = lax.broadcasted_iota(jnp.int32, alive.shape, 0)
    alive[...] = jnp.where((ext_row >= TAIL) | (device > 0), 1.0, 0.0)


def score_head(head, query_ref, key_blocks, pair_tail_ref, pair_keys_ref,
               keys_ext, pair_query, pair_ext, scores, tops):
    length = query_ref.shape[0]
    blocks = len(key_blocks)
    cols = head_columns(head)
    pair_ext[0:TAIL, :] = pair_tail_ref[:, cols].astype(jnp.float32)
    pair_ext[TAIL:, :] = pair_keys_ref[:, cols].astype(jnp.float32)
    for place, block in enumerate(key_blocks):
        keys_ext[place * length:(place + 1) * length, :HEAD_DIM] = block[:, cols]
    query = query_ref[:, cols].astype(jnp.float32) * SCALE
    for offset in range(WIN_PAIRS):
        pair_query[offset * length:(offset + 1) * length, :HEAD_DIM] = (
            query * pair_ext[TAIL - offset:TAIL - offset + length, :]
        ).astype(jnp.bfloat16)
    top = None
    total = blocks * length
    for start in range(0, total, 256):
        size = min(256, total - start)
        part = lax.dot_general(
            pair_query[...], keys_ext[start:start + size, :],
            (((1,), (1,)), ((), ())), preferred_element_type=jnp.float32,
        )
        scores[:, start:start + size] = part
        for lane in range(0, size, 128):
            for offset in range(WIN_PAIRS):
                tile = part[offset * length:(offset + 1) * length, lane:lane + 128]
                top = tile if top is None else jnp.maximum(top, tile)
    tops[...] = jnp.broadcast_to(jnp.max(top, axis=1, keepdims=True), tops.shape)


def value_head(head, value_blocks, pair_tail_ref, pair_values_ref,
               values_ext, pair_ext, alive, scores, tops, weights, out_ref):
    length = tops.shape[0]
    blocks = len(value_blocks)
    cols = head_columns(head)
    pair_ext[0:TAIL, :] = pair_tail_ref[:, cols].astype(jnp.float32)
    pair_ext[TAIL:, :] = pair_values_ref[:, cols].astype(jnp.float32)
    for place, block in enumerate(value_blocks):
        values_ext[place * length:(place + 1) * length, :HEAD_DIM] = block[:, cols]
    top = tops[...]
    for offset in range(WIN_PAIRS):
        rows = slice(offset * length, (offset + 1) * length)
        for place in range(blocks):
            lanes = slice(place * length, (place + 1) * length)
            weights[rows, lanes] = jnp.exp2((scores[rows, lanes] - top).astype(jnp.bfloat16))
    product = jnp.dot(weights[...], values_ext[...], preferred_element_type=jnp.float32)
    number = jnp.zeros((length, HEAD_DIM), jnp.float32)
    total = jnp.zeros((length, HEAD_DIM), jnp.float32)
    for offset in range(WIN_PAIRS):
        rows = slice(offset * length, (offset + 1) * length)
        near = slice(TAIL - offset, TAIL - offset + length)
        number += product[rows, :HEAD_DIM] * pair_ext[near, :]
        total += product[rows, HEAD_DIM:] * alive[near, :]
    out_ref[:, cols] = (number / total).astype(out_ref.dtype)


def attention_kernel(query, k0, k1, k2, k3, k4, v0, v1, v2, v3, v4,
                     key_tail, pair_keys, value_tail, pair_values, out,
                     keys_ext, pair_query, values_ext, key_ext, value_ext, alive,
                     scores_a, scores_b, tops_a, tops_b, weights):
    length = query.shape[0]
    heads = query.shape[1] // HEAD_DIM
    key_blocks = (k0, k1, k2, k3, k4)
    value_blocks = (v0, v1, v2, v3, v4)
    device = lax.axis_index("wide")
    build_masks(device, length, len(key_blocks), keys_ext, pair_query, values_ext, alive)

    def score(head, scores, tops):
        score_head(head, query, key_blocks, key_tail, pair_keys,
                   keys_ext, pair_query, key_ext, scores, tops)

    def value(head, scores, tops):
        value_head(head, value_blocks, value_tail, pair_values,
                   values_ext, value_ext, alive, scores, tops, weights, out)

    score(0, scores_a, tops_a)

    def pair(step, carry):
        head = step * 2
        score(head + 1, scores_b, tops_b)
        value(head, scores_a, tops_a)
        score(jnp.minimum(head + 2, heads - 1), scores_a, tops_a)
        value(head + 1, scores_b, tops_b)
        return carry

    lax.fori_loop(0, heads // 2, pair, 0)


def attention(query, key_blocks, value_blocks, key_tail, pair_keys, value_tail, pair_values,
              chunk, width):
    length = query.shape[0]
    blocks = len(key_blocks)
    whole = pl.BlockSpec((length, width), lambda i: (0, chunk))
    sliced = pl.BlockSpec((length, width), lambda i: (0, 0))
    tail = pl.BlockSpec((TAIL, width), lambda i: (0, chunk))
    rows = WIN_PAIRS * length
    keys = blocks * length
    heads = width // HEAD_DIM
    return pl.pallas_call(
        attention_kernel,
        grid=(1,),
        out_shape=jax.ShapeDtypeStruct((length, width), jnp.bfloat16),
        in_specs=[whole] + [sliced] * (2 * blocks) + [tail, whole, tail, whole],
        out_specs=sliced,
        scratch_shapes=[
            pltpu.VMEM((keys, 2 * HEAD_DIM), jnp.bfloat16),
            pltpu.VMEM((rows, 2 * HEAD_DIM), jnp.bfloat16),
            pltpu.VMEM((keys, 2 * HEAD_DIM), jnp.bfloat16),
            pltpu.VMEM((TAIL + length, HEAD_DIM), jnp.float32),
            pltpu.VMEM((TAIL + length, HEAD_DIM), jnp.float32),
            pltpu.VMEM((TAIL + length, HEAD_DIM), jnp.float32),
            pltpu.VMEM((rows, keys), jnp.float32),
            pltpu.VMEM((rows, keys), jnp.float32),
            pltpu.VMEM((length, HEAD_DIM), jnp.float32),
            pltpu.VMEM((length, HEAD_DIM), jnp.float32),
            pltpu.VMEM((rows, keys), jnp.bfloat16),
        ],
        compiler_params=pltpu.CompilerParams(vmem_limit_bytes=40 * 2**20),
        cost_estimate=pl.CostEstimate(
            flops=heads * 8 * rows * keys * HEAD_DIM,
            bytes_accessed=(2 * blocks + 4) * length * width * 2,
            transcendentals=heads * rows * keys,
        ),
    )(query, *key_blocks, *value_blocks, key_tail, pair_keys, value_tail, pair_values)


def spread_blocks(keys, values, devices, device):
    def move(arrays, pairs):
        return lax.ppermute(arrays, "wide", pairs)

    own = (keys, values)
    far = move(own, [(i, i + 4) for i in range(devices - 4)])
    low = lax.rem(device, 4) < 2
    sent = tuple(jnp.where(low, a, b) for a, b in zip(own, far))
    middle = move(sent, [(i, i ^ 2) for i in range(devices)])
    even = lax.rem(device, 2) == 0
    sent = tuple(jnp.where(even, a, b) for a, b in zip(own, far))
    swap = [(i, i ^ 1) for i in range(devices)]
    first = move(sent, swap)
    second = move(middle, swap)
    return tuple(zip(far, middle, first, second, own))


def on_device(
    queries,
    first_keys,
    first_values,
    second_keys,
    second_values,
    out_weight,
    norm_gain,
    gate_weight,
    up_weight,
    down_weight,
    routes,
    route_weights,
):
    length = queries.shape[0]
    feature_width = queries.shape[1]
    head_count = feature_width // HEAD_DIM
    chunks = math.gcd(head_count // 2, 4)
    chunk_width = feature_width // chunks
    device = lax.axis_index("wide")
    devices = lax.axis_size("wide")
    assert length * 4 == WIN_KEYS and devices % 4 == 0
    full_weight = lax.all_gather(out_weight, "wide", axis=0, tiled=True)
    key_tail, value_tail = lax.ppermute(
        (second_keys[length - TAIL:], second_values[length - TAIL:]),
        "wide",
        [(i, i + 1) for i in range(devices - 1)],
    )
    key_tail = jnp.where(device == 0, second_keys[0:1], key_tail)
    pieces = []
    for chunk in range(chunks):
        cols = slice(chunk * chunk_width, (chunk + 1) * chunk_width)
        key_blocks, value_blocks = spread_blocks(
            first_keys[:, cols], first_values[:, cols], devices, device
        )
        pieces.append(
            attention(queries, key_blocks, value_blocks, key_tail, second_keys,
                      value_tail, second_values, chunk, chunk_width)
        )
    attended = jnp.concatenate(pieces, axis=1)
    model_width = out_weight.shape[1]
    projected32 = jnp.dot(
        attended,
        full_weight,
        preferred_element_type=jnp.float32,
    )
    projected = projected32.astype(jnp.bfloat16)
    wide_proj = projected.astype(jnp.float32)
    normed = (
        wide_proj
        * lax.rsqrt(jnp.mean(wide_proj * wide_proj, axis=1, keepdims=True) + 1e-06)
        * norm_gain
    ).astype(jnp.bfloat16)
    local_experts = gate_weight.shape[0]
    flight = local_experts * devices
    slot_count = flight * CAP
    route_count = routes.shape[1]
    flat_routes = routes.reshape(-1)
    entry = jnp.arange(flat_routes.shape[0], dtype=jnp.int32)
    same = (flat_routes[:, None] == flat_routes[None, :]) & (entry[None, :] < entry[:, None])
    ranking = jnp.sum(same.astype(jnp.int32), axis=1)
    in_flight = flat_routes < flight
    target = jnp.where(in_flight, flat_routes * CAP + ranking, slot_count)
    chooser = target[None, :] == jnp.arange(slot_count, dtype=jnp.int32)[:, None]
    token_chooser = jnp.any(chooser.reshape(slot_count, length, route_count), axis=2)
    outgoing = jnp.dot(
        token_chooser.astype(jnp.bfloat16), normed, preferred_element_type=jnp.float32
    ).astype(jnp.bfloat16)
    outgoing = outgoing.reshape(devices, local_experts, CAP, model_width)
    arrived = lax.all_to_all(outgoing, "wide", split_axis=0, concat_axis=0, tiled=True)
    sources, experts_here, kept_slots, row_width = arrived.shape
    expert_rows = arrived.transpose(1, 0, 2, 3).reshape(
        experts_here, sources * kept_slots, row_width
    )
    gate_proj = jnp.einsum(
        "erd,edf->erf", expert_rows, gate_weight, preferred_element_type=jnp.float32
    )
    upward = jnp.einsum("erd,edf->erf", expert_rows, up_weight, preferred_element_type=jnp.float32)
    hidden = (jax.nn.silu(gate_proj) * upward).astype(jnp.bfloat16)
    result = jnp.einsum(
        "erf,efd->erd", hidden, down_weight, preferred_element_type=jnp.float32
    ).astype(jnp.bfloat16)
    finished = result.reshape(experts_here, sources, kept_slots, row_width).transpose(1, 0, 2, 3)
    returned = lax.all_to_all(finished, "wide", split_axis=0, concat_axis=0, tiled=True).reshape(
        slot_count, model_width
    )
    picked = jnp.take(returned, jnp.minimum(target, slot_count - 1), axis=0).astype(jnp.float32)
    route_scale = jnp.where(in_flight, route_weights.reshape(-1), jnp.float32(0.0))
    expert_sum = jnp.sum(
        (picked * route_scale[:, None]).reshape(length, route_count, model_width), axis=1
    )
    return (wide_proj + expert_sum).astype(jnp.bfloat16)


def solution(mesh):
    in_specs = (
        P(("groups", "wide"), None),
        P(("groups", "wide"), None),
        P(("groups", "wide"), None),
        P(("groups", "wide"), None),
        P(("groups", "wide"), None),
        P("wide", None),
        P(),
        P("wide", None, None),
        P("wide", None, None),
        P("wide", None, None),
        P(("groups", "wide"), None),
        P(("groups", "wide"), None),
    )
    out_specs = P(("groups", "wide"), None)
    return jax.shard_map(
        on_device, mesh=mesh, in_specs=in_specs, out_specs=out_specs, check_vma=False
    )
```

time: 711 us -> 281 us (0.40)
  local copies, waits for them, and re-layouts: 183 us -> 14.7 us
  matrix products: 176 us -> 19.3 us
  other arithmetic: 98.1 us -> 9.24 us
  starting transfers between devices: 159 us -> 88.5 us
  Pallas kernels: 0 us -> 55.4 us
  waiting for transfers between devices: 13.7 us -> 61.9 us
  blocking collectives: 62.6 us -> 17.2 us
    dot_general x17 -> x1, matrix products: 165 us -> 8.19 us  [on_device(): jnp.dot(attended, full_weight, preferred_element_type=jnp.float32)]
    while x208 -> x0, local copies, waits for them, and re-layouts: 116 us -> none
    reduce_sum x9 -> x1, other arithmetic: 70.7 us -> 0.26 us  [on_device(): ranking = jnp.sum(same.astype(jnp.int32), axis=1)]
    ppermute x10 -> x34, starting transfers between devices: 154 us -> 84.5 us  [the longest x32 81.9 us: move(): return lax.ppermute(arrays, 'wide', pairs)]
    pallas_call x0 -> x4, Pallas kernels: none -> 55.4 us  [attention(): pl.pallas_call(attention_kernel, grid=(1,), out_shape=jax.ShapeDtypeStruc...]
    all_to_all x1, blocking collectives: 62.6 us -> 17.2 us  [on_device(): lax.all_to_all(outgoing, 'wide', split_axis=0, concat_axis=0, tiled=True)]
    ppermute x10 -> x34, waiting for transfers between devices: 0.03 us -> 37.3 us  [the longest x32 37.3 us: move(): return lax.ppermute(arrays, 'wide', pairs)]
    dynamic_update_slice x20 -> x0, local copies, waits for them, and re-layouts: 16.8 us -> none  [the longest x8 7.26 us: relay_step(): lax.dynamic_update_slice_in_dim(keys_buffer, moving_keys, place_row, 0)]
  transfers between devices with their start and end apart: 12 -> 36, of which waited for: 1 -> 12; matrix products, arithmetic and copies ran while one was open for 58% -> 3% of each run, Pallas kernels for 0% -> 20%
where the time goes in v1:
time: 281 us; the launch traced here: 280 us
  starting transfers between devices  88.5 us (31%)
  waiting for transfers between devices  61.9 us (22%)
  Pallas kernels  55.4 us (20%)
  matrix products  19.3 us (7%)
  blocking collectives  17.2 us (6%)
  local copies, waits for them, and re-layouts  14.7 us (5%)
  between operations  13.9 us (5%)
  other arithmetic  9.24 us (3%)
    ppermute x32, starting transfers between devices, move(): return lax.ppermute(arrays, 'wide', pairs)  81.9 us
    pallas_call x4, Pallas kernels, attention(): pl.pallas_call(attention_kernel, grid=(1,), out_shape=jax.ShapeDtypeStruc...  55.4 us
    ppermute x32, waiting for transfers between devices, move(): return lax.ppermute(arrays, 'wide', pairs)  37.3 us
    all_to_all x1, blocking collectives, on_device(): lax.all_to_all(outgoing, 'wide', split_axis=0, concat_axis=0, tiled=True)  17.2 us
    all_to_all x1, waiting for transfers between devices, on_device(): lax.all_to_all(finished, 'wide', split_axis=0, concat_axis=0, tiled=True)  13.7 us
    all_gather x1, waiting for transfers between devices, on_device(): full_weight = lax.all_gather(out_weight, 'wide', axis=0, tiled=True)  10.2 us
    dot_general x1, matrix products, on_device(): jnp.dot(attended, full_weight, preferred_element_type=jnp.float32)  8.19 us
    dot_general x1, matrix products, on_device(): jnp.einsum('erf,efd->erd', hidden, down_weight, preferred_element_type=jn...  6.86 us
  transfers between devices with their start and end apart: 36, of which 12 were waited for; matrix products, arithmetic and copies ran while one was open for 3% of the time, Pallas kernels for 20%

profile of v1, /device:TPU:0, one launch (start us, length us, event | category | flops | bytes accessed | tf_op | source)
XLA Modules:
  0.0 280.2 jit_solution(13559643320904950633)
XLA Ops:
  8.2 4.9 %collective-permute-start.4 = (bf16[128,1024]{1,0:T(8,128)(2,1)S(1)}, bf16[128,1024]{1,0:T(8,128)(2,1)S(1)}, u32[]{:S(2)}, u32[]{:S(2)}) collective-permute-start(bf16[128,1024]{1,0:T(8,128)(2,1)S(1)} %slice.34.v4), channel_id=1, source_target_pairs={{0,4},{1,5},{2,6},{3,7},{4,8},{5,9},{6,10},{7,11},{8,12},{9,13},{1... | collective-permute-start | bytes 786440 | tf_op jit(solution)/shard_map/ppermute | solution.py:176
  14.2 3.5 %collective-permute-start = (bf16[128,1024]{1,0:T(8,128)(2,1)S(1)}, bf16[128,1024]{1,0:T(8,128)(2,1)S(1)}, u32[]{:S(2)}, u32[]{:S(2)}) collective-permute-start(bf16[128,1024]{1,0:T(8,128)(2,1)S(1)} %slice.33.k4), channel_id=1, source_target_pairs={{0,4},{1,5},{2,6},{3,7},{4,8},{5,9},{6,10},{7,11},{8,12},{9,13},{1... | collective-permute-start | bytes 786440 | tf_op jit(solution)/shard_map/ppermute | solution.py:176
  17.7 1.6 slice.36
  19.2 1.3 collective-permute-start.8
  24.4 1.3 broadcast_select_fusion.6
  25.7 2.2 collective-permute-start.5
  27.9 3.5 %collective-permute-start.14 = (bf16[128,1024]{1,0:T(8,128)(2,1)S(1)}, bf16[128,1024]{1,0:T(8,128)(2,1)S(1)}, u32[]{:S(2)}, u32[]{:S(2)}) collective-permute-start(bf16[128,1024]{1,0:T(8,128)(2,1)S(1)} %get-tuple-element.24.v4), channel_id=1, source_target_pairs={{0,4},{1,5},{2,6},{3,7},{4,8},{5,9},{6,10},{7,11},{8,12},{9,13},{1... | collective-permute-start | bytes 786440 | tf_op jit(solution)/shard_map/ppermute | solution.py:176
  31.4 2.0 collective-permute-start.22
  33.4 2.2 collective-permute-start.30
  35.7 7.9 %collective-permute-done.14.v0 = bf16[128,1024]{1,0:T(8,128)(2,1)S(1)} collective-permute-done((bf16[128,1024]{1,0:T(8,128)(2,1)S(1)}, bf16[128,1024]{1,0:T(8,128)(2,1)S(1)}, u32[]{:S(2)}, u32[]{:S(2)}) %collective-permute-start.14) | collective-permute-done | bytes 262176 | tf_op jit(solution)/shard_map/ppermute | solution.py:176
  43.6 6.2 %collective-permute-start.10 = (bf16[128,1024]{1,0:T(8,128)(2,1)S(1)}, bf16[128,1024]{1,0:T(8,128)(2,1)S(1)}, u32[]{:S(2)}, u32[]{:S(2)}) collective-permute-start(bf16[128,1024]{1,0:T(8,128)(2,1)S(1)} %get-tuple-element.27.k4), channel_id=1, source_target_pairs={{0,4},{1,5},{2,6},{3,7},{4,8},{5,9},{6,10},{7,11},{8,12},{9,13},{1... | collective-permute-start | bytes 786440 | tf_op jit(solution)/shard_map/ppermute | solution.py:176
  49.9 5.0 %collective-permute-done.22.v0 = bf16[128,1024]{1,0:T(8,128)(2,1)S(1)} collective-permute-done((bf16[128,1024]{1,0:T(8,128)(2,1)S(1)}, bf16[128,1024]{1,0:T(8,128)(2,1)S(1)}, u32[]{:S(2)}, u32[]{:S(2)}) %collective-permute-start.22) | collective-permute-done | bytes 262176 | tf_op jit(solution)/shard_map/ppermute | solution.py:176
  54.9 10.3 %collective-permute-start.18 = (bf16[128,1024]{1,0:T(8,128)(2,1)S(1)}, bf16[128,1024]{1,0:T(8,128)(2,1)S(1)}, u32[]{:S(2)}, u32[]{:S(2)}) collective-permute-start(bf16[128,1024]{1,0:T(8,128)(2,1)S(1)} %get-tuple-element.29.k4), channel_id=1, source_target_pairs={{0,4},{1,5},{2,6},{3,7},{4,8},{5,9},{6,10},{7,11},{8,12},{9,13},{1... | collective-permute-start | bytes 786440 | tf_op jit(solution)/shard_map/ppermute | solution.py:176
  66.1 9.7 %collective-permute-start.26 = (bf16[128,1024]{1,0:T(8,128)(2,1)S(1)}, bf16[128,1024]{1,0:T(8,128)(2,1)S(1)}, u32[]{:S(2)}, u32[]{:S(2)}) collective-permute-start(bf16[128,1024]{1,0:T(8,128)(2,1)S(1)} %get-tuple-element.28.k4), channel_id=1, source_target_pairs={{0,4},{1,5},{2,6},{3,7},{4,8},{5,9},{6,10},{7,11},{8,12},{9,13},{1... | collective-permute-start | bytes 786440 | tf_op jit(solution)/shard_map/ppermute | solution.py:176
  75.9 1.3 collective-permute-start.9
  77.3 3.3 %collective-permute-start.1 = (bf16[128,1024]{1,0:T(8,128)(2,1)S(1)}, bf16[128,1024]{1,0:T(8,128)(2,1)S(1)}, u32[]{:S(2)}, u32[]{:S(2)}) collective-permute-start(bf16[128,1024]{1,0:T(8,128)(2,1)S(1)} %get-tuple-element.11), channel_id=1, source_target_pairs={{0,2},{1,3},{2,0},{3,1},{4,6},{5,7},{6,4},{7,5},{8,10},{9,11},{10,... | collective-permute-start | bytes 786440 | tf_op jit(solution)/shard_map/ppermute | solution.py:176
  80.6 3.3 %collective-permute-start.6 = (bf16[128,1024]{1,0:T(8,128)(2,1)S(1)}, bf16[128,1024]{1,0:T(8,128)(2,1)S(1)}, u32[]{:S(2)}, u32[]{:S(2)}) collective-permute-start(bf16[128,1024]{1,0:T(8,128)(2,1)S(1)} %get-tuple-element.8), channel_id=1, source_target_pairs={{0,1},{1,0},{2,3},{3,2},{4,5},{5,4},{6,7},{7,6},{8,9},{9,8},{10,11... | collective-permute-start | bytes 786440 | tf_op jit(solution)/shard_map/ppermute | solution.py:176
  83.9 2.6 collective-permute-done.18.k0
  86.5 5.3 %collective-permute-done.26.k0 = bf16[128,1024]{1,0:T(8,128)(2,1)S(1)} collective-permute-done((bf16[128,1024]{1,0:T(8,128)(2,1)S(1)}, bf16[128,1024]{1,0:T(8,128)(2,1)S(1)}, u32[]{:S(2)}, u32[]{:S(2)}) %collective-permute-start.26) | collective-permute-done | bytes 262176 | tf_op jit(solution)/shard_map/ppermute | solution.py:176
  91.9 3.1 %collective-permute-start.15 = (bf16[128,1024]{1,0:T(8,128)(2,1)S(1)}, bf16[128,1024]{1,0:T(8,128)(2,1)S(1)}, u32[]{:S(2)}, u32[]{:S(2)}) collective-permute-start(bf16[128,1024]{1,0:T(8,128)(2,1)S(1)} %get-tuple-element.13), channel_id=1, source_target_pairs={{0,2},{1,3},{2,0},{3,1},{4,6},{5,7},{6,4},{7,5},{8,10},{9,11},{10,... | collective-permute-start | bytes 786440 | tf_op jit(solution)/shard_map/ppermute | solution.py:176
  95.0 3.2 %collective-permute-start.16 = (bf16[128,1024]{1,0:T(8,128)(2,1)S(1)}, bf16[128,1024]{1,0:T(8,128)(2,1)S(1)}, u32[]{:S(2)}, u32[]{:S(2)}) collective-permute-start(bf16[128,1024]{1,0:T(8,128)(2,1)S(1)} %get-tuple-element.12), channel_id=1, source_target_pairs={{0,1},{1,0},{2,3},{3,2},{4,5},{5,4},{6,7},{7,6},{8,9},{9,8},{10,11... | collective-permute-start | bytes 786440 | tf_op jit(solution)/shard_map/ppermute | solution.py:176
  99.0 1.6 collective-permute-done.3.k3
  100.6 1.7 collective-permute-start.23
  102.4 4.2 %collective-permute-done.15.v1 = bf16[128,1024]{1,0:T(8,128)(2,1)S(1)} collective-permute-done((bf16[128,1024]{1,0:T(8,128)(2,1)S(1)}, bf16[128,1024]{1,0:T(8,128)(2,1)S(1)}, u32[]{:S(2)}, u32[]{:S(2)}) %collective-permute-start.15) | collective-permute-done | bytes 262176 | tf_op jit(solution)/shard_map/ppermute | solution.py:176
  106.6 4.2 %collective-permute-start.24 = (bf16[128,1024]{1,0:T(8,128)(2,1)S(1)}, bf16[128,1024]{1,0:T(8,128)(2,1)S(1)}, u32[]{:S(2)}, u32[]{:S(2)}) collective-permute-start(bf16[128,1024]{1,0:T(8,128)(2,1)S(1)} %get-tuple-element.31), channel_id=1, source_target_pairs={{0,1},{1,0},{2,3},{3,2},{4,5},{5,4},{6,7},{7,6},{8,9},{9,8},{10,11... | collective-permute-start | bytes 786440 | tf_op jit(solution)/shard_map/ppermute | solution.py:176
  110.8 1.7 collective-permute-start.19
  112.5 5.3 %collective-permute-done.11.k1 = bf16[128,1024]{1,0:T(8,128)(2,1)S(1)} collective-permute-done((bf16[128,1024]{1,0:T(8,128)(2,1)S(1)}, bf16[128,1024]{1,0:T(8,128)(2,1)S(1)}, u32[]{:S(2)}, u32[]{:S(2)}) %collective-permute-start.11) | collective-permute-done | bytes 262176 | tf_op jit(solution)/shard_map/ppermute | solution.py:176
  117.8 4.2 %collective-permute-start.17 = (bf16[128,1024]{1,0:T(8,128)(2,1)S(1)}, bf16[128,1024]{1,0:T(8,128)(2,1)S(1)}, u32[]{:S(2)}, u32[]{:S(2)}) collective-permute-start(bf16[128,1024]{1,0:T(8,128)(2,1)S(1)} %collective-permute-done.15.v1), channel_id=1, source_target_pairs={{0,1},{1,0},{2,3},{3,2},{4,5},{5,4},{6,7},{7,6},{8,9},{9,8},{10,11... | collective-permute-start | bytes 786440 | tf_op jit(solution)/shard_map/ppermute | solution.py:176
  122.0 13.8 %shard_map.118 = bf16[128,1024]{1,0:T(8,128)(2,1)S(1)} custom-call(bf16[128,4096]{1,0:T(8,128)(2,1)S(1)} %copy-done.2, bf16[128,1024]{1,0:T(8,128)(2,1)S(1)} %collective-permute-done.k0, bf16[128,1024]{1,0:T(8,128)(2,1)S(1)} %collective-permute-done.1.k1, bf16[128,1024]{1,0:T(8,128)(2,1)S(1)} %collective-permute-done.2.k2, ...), custom_call_target="tpu_custom_call" | custom-call | flops 8053063680 | bytes 3670016 | tf_op jit(solution)/shard_map/pallas_call | solution.py:146
  136.4 1.7 collective-permute-start.31
  138.1 2.1 collective-permute-done.19.k1
  140.3 2.4 collective-permute-start.27
  142.7 3.3 %collective-permute-start.25 = (bf16[128,1024]{1,0:T(8,128)(2,1)S(1)}, bf16[128,1024]{1,0:T(8,128)(2,1)S(1)}, u32[]{:S(2)}, u32[]{:S(2)}) collective-permute-start(bf16[128,1024]{1,0:T(8,128)(2,1)S(1)} %collective-permute-done.23.v1), channel_id=1, source_target_pairs={{0,1},{1,0},{2,3},{3,2},{4,5},{5,4},{6,7},{7,6},{8,9},{9,8},{10,11... | collective-permute-start | bytes 786440 | tf_op jit(solution)/shard_map/ppermute | solution.py:176
  146.0 13.8 %shard_map.119 = bf16[128,1024]{1,0:T(8,128)(2,1)S(1)} custom-call(bf16[128,4096]{1,0:T(8,128)(2,1)S(1)} %copy-done.2, bf16[128,1024]{1,0:T(8,128)(2,1)S(1)} %collective-permute-done.10.k0, bf16[128,1024]{1,0:T(8,128)(2,1)S(1)} %collective-permute-done.11.k1, bf16[128,1024]{1,0:T(8,128)(2,1)S(1)} %collective-permute-done.12.k2, ...), custom_call_target="tpu_custom_call" | custom-call | flops 8053063680 | bytes 3670016 | tf_op jit(solution)/shard_map/pallas_call | solution.py:146
  160.4 2.3 collective-permute-done.27.k1
  162.7 3.2 %collective-permute-start.33 = (bf16[128,1024]{1,0:T(8,128)(2,1)S(1)}, bf16[128,1024]{1,0:T(8,128)(2,1)S(1)}, u32[]{:S(2)}, u32[]{:S(2)}) collective-permute-start(bf16[128,1024]{1,0:T(8,128)(2,1)S(1)} %collective-permute-done.31.v1), channel_id=1, source_target_pairs={{0,1},{1,0},{2,3},{3,2},{4,5},{5,4},{6,7},{7,6},{8,9},{9,8},{10,11... | collective-permute-start | bytes 786440 | tf_op jit(solution)/shard_map/ppermute | solution.py:176
  166.0 14.0 %shard_map.120 = bf16[128,1024]{1,0:T(8,128)(2,1)S(1)} custom-call(bf16[128,4096]{1,0:T(8,128)(2,1)S(1)} %copy-done.2, bf16[128,1024]{1,0:T(8,128)(2,1)S(1)} %collective-permute-done.18.k0, bf16[128,1024]{1,0:T(8,128)(2,1)S(1)} %collective-permute-done.19.k1, bf16[128,1024]{1,0:T(8,128)(2,1)S(1)} %collective-permute-done.20.k2, ...), custom_call_target="tpu_custom_call" | custom-call | flops 8053063680 | bytes 3670016 | tf_op jit(solution)/shard_map/pallas_call | solution.py:146
  180.0 13.8 %shard_map.121 = bf16[128,1024]{1,0:T(8,128)(2,1)S(1)} custom-call(bf16[128,4096]{1,0:T(8,128)(2,1)S(1)} %copy-done.2, bf16[128,1024]{1,0:T(8,128)(2,1)S(1)} %collective-permute-done.26.k0, bf16[128,1024]{1,0:T(8,128)(2,1)S(1)} %collective-permute-done.27.k1, bf16[128,1024]{1,0:T(8,128)(2,1)S(1)} %collective-permute-done.28.k2, ...), custom_call_target="tpu_custom_call" | custom-call | flops 8053063680 | bytes 3670016 | tf_op jit(solution)/shard_map/pallas_call | solution.py:146
  193.8 10.2 %all-gather.2.cloned.1.call-done = bf16[4096,2048]{1,0:T(8,128)(2,1)} async-done(((bf16[256,2048]{1,0:T(8,128)(2,1)}), bf16[4096,2048]{1,0:T(8,128)(2,1)}) %all-gather.2.cloned.1.call-update) | async-done | bytes 16777232 | tf_op jit(solution)/shard_map/all_gather | solution.py:213
  204.0 8.2 %multiply_reduce_fusion.1 = (f32[128]{0:T(128)S(1)}, f32[128,2048]{1,0:T(8,128)S(1)}) fusion(bf16[4096,2048]{1,0:T(8,128)(2,1)} %all-gather.2.cloned.1.call-done, bf16[128,1024]{1,0:T(8,128)(2,1)S(1)} %shard_map.121, bf16[128,1024]{1,0:T(8,128)(2,1)S(1)} %shard_map.120, bf16[128,1024]{1,0:T(8,128)(2,1)S(1)} %shard_map.119, bf16[128,1024]{1,0:T(8,128)(2,1)S(1)} %shard_map.118), kind=kOutput, calls=%fused_computation.17 | convolution fusion | flops 2152726528 | bytes 18874880 | tf_op jit(solution)/shard_map/dot_general | solution.py:232
  213.8 17.2 %all_to_all.10 = bf16[16,2,4,2048]{3,2,1,0:T(4,128)(2,1)S(1)} all-to-all(bf16[16,2,4,2048]{3,2,1,0:T(4,128)(2,1)S(1)} %reshape.119), channel_id=1, replica_groups=mesh['groups'=2,'wide'=16] {'wide'}, dimensions={0} | all-to-all | bytes 1048576 | tf_op jit(solution)/shard_map/all_to_all | solution.py:260
  231.4 3.9 %fusion.21 = f32[2,64,768]{2,1,0:T(8,128)S(1)} fusion(bf16[2,64,2048]{2,1,0:T(8,128)(2,1)S(1)} %reshape.120, bf16[2,2048,768]{2,1,0:T(8,128)(2,1)} %param.19), kind=kOutput, calls=%fused_computation.61 | convolution fusion | flops 402653184 | bytes 7208960 | tf_op jit(solution)/shard_map/erd,edf->erf/dot_general | solution.py:265
  235.3 6.9 %convolution_convert_fusion = bf16[2,64,2048]{2,1,0:T(8,128)(2,1)S(1)} fusion(bf16[2,768,2048]{2,1,0:T(8,128)(2,1)} %param.21, bf16[2,64,2048]{2,1,0:T(8,128)(2,1)S(1)} %reshape.120, bf16[2,2048,768]{2,1,0:T(8,128)(2,1)} %param.20, f32[2,64,768]{2,1,0:T(8,128)S(1)} %fusion.21), kind=kOutput, calls=%fused_computation.2 | convolution fusion | flops 806158336 | bytes 14024704 | tf_op jit(solution)/shard_map/erf,efd->erd/dot_general | solution.py:270
  243.4 4.1 %all-to-all-start.1 = ((bf16[16,2,4,2048]{3,2,1,0:T(4,128)(2,1)}), bf16[16,2,4,2048]{3,2,1,0:T(4,128)(2,1)S(1)}, u32[]{:S(2)}, u32[]{:S(2)}) async-start(bf16[16,2,4,2048]{3,2,1,0:T(4,128)(2,1)} %bitcast.12), calls=%async_computation.1 | async-start | bytes 1048576 | tf_op jit(solution)/shard_map/all_to_all | solution.py:274
  248.3 13.7 %all-to-all-done.1 = bf16[16,2,4,2048]{3,2,1,0:T(4,128)(2,1)S(1)} async-done(((bf16[16,2,4,2048]{3,2,1,0:T(4,128)(2,1)}), bf16[16,2,4,2048]{3,2,1,0:T(4,128)(2,1)S(1)}, u32[]{:S(2)}, u32[]{:S(2)}) %all-to-all-start.1) | async-done | bytes 524320 | tf_op jit(solution)/shard_map/all_to_all | solution.py:274
  262.0 2.5 gather_fusion
  264.5 2.2 gather.7
  266.8 5.6 %multiply_reduce_fusion = f32[128,2048]{1,0:T(8,128)S(1)} fusion(f32[128,4]{1,0:T(8,128)S(1)} %copy.44, bf16[128,4,2048]{2,1,0:T(4,128)(2,1)} %gather.7, pred[128,4]{1,0:T(8,128)(4,1)S(1)} %copy.39), kind=kLoop, calls=%fused_computation.1 | loop fusion | flops 3932160 | bytes 3148288 | tf_op jit(solution)/shard_map/reduce_sum | solution.py:279
  (92 shorter events, 14.8 us)
Async XLA Ops:
  6.5 69.3 %copy-start.3 = (bf16[128,4096]{1,0:T(8,128)(2,1)S(1)}, bf16[128,4096]{1,0:T(8,128)(2,1)}, u32[]{:S(2)}) copy-start(bf16[128,4096]{1,0:T(8,128)(2,1)} %param.14) | copy-start | bytes 3145732
  6.5 29.1 %copy-start.4 = (bf16[128,4096]{1,0:T(8,128)(2,1)S(1)}, bf16[128,4096]{1,0:T(8,128)(2,1)}, u32[]{:S(2)}) copy-start(bf16[128,4096]{1,0:T(8,128)(2,1)} %param.13) | copy-start | bytes 3145732
  6.5 197.5 %all-gather.2.cloned.1.call-start = ((), (), s32[]{:S(2)}) async-start(), calls=%async_computation.2 | async-start | bytes 17825792 | tf_op jit(solution)/shard_map/all_gather | solution.py:213
  8.2 16.2 %collective-permute-start.4 = (bf16[128,1024]{1,0:T(8,128)(2,1)S(1)}, bf16[128,1024]{1,0:T(8,128)(2,1)S(1)}, u32[]{:S(2)}, u32[]{:S(2)}) collective-permute-start(bf16[128,1024]{1,0:T(8,128)(2,1)S(1)} %slice.34.v4), channel_id=1, source_target_pairs={{0,4},{1,5},{2,6},{3,7},{4,8},{5,9},{6,10},{7,11},{8,12},{9,13},{1... | collective-permute-start | bytes 786440 | tf_op jit(solution)/shard_map/ppermute | solution.py:176
  14.2 19.2 %collective-permute-start = (bf16[128,1024]{1,0:T(8,128)(2,1)S(1)}, bf16[128,1024]{1,0:T(8,128)(2,1)S(1)}, u32[]{:S(2)}, u32[]{:S(2)}) collective-permute-start(bf16[128,1024]{1,0:T(8,128)(2,1)S(1)} %slice.33.k4), channel_id=1, source_target_pairs={{0,4},{1,5},{2,6},{3,7},{4,8},{5,9},{6,10},{7,11},{8,12},{9,13},{1... | collective-permute-start | bytes 786440 | tf_op jit(solution)/shard_map/ppermute | solution.py:176
  19.2 56.7 %collective-permute-start.8 = (bf16[16,4096]{1,0:T(8,128)(2,1)}, bf16[16,4096]{1,0:T(8,128)(2,1)S(1)}, u32[]{:S(2)}, u32[]{:S(2)}) collective-permute-start(bf16[16,4096]{1,0:T(8,128)(2,1)} %slice.36), channel_id=1, source_target_pairs={{0,1},{1,2},{2,3},{3,4},{4,5},{5,6},{6,7},{7,8},{8,9},{9,10},{10,1... | collective-permute-start | bytes 393224 | tf_op jit(solution)/shard_map/ppermute | solution.py:214
  25.7 51.5 %collective-permute-start.5 = (bf16[128,1024]{1,0:T(8,128)(2,1)S(1)}, bf16[128,1024]{1,0:T(8,128)(2,1)S(1)}, u32[]{:S(2)}, u32[]{:S(2)}) collective-permute-start(bf16[128,1024]{1,0:T(8,128)(2,1)S(1)} %get-tuple-element.9), channel_id=1, source_target_pairs={{0,2},{1,3},{2,0},{3,1},{4,6},{5,7},{6,4},{7,5},{8,10},{9,11},{10,... | collective-permute-start | bytes 786440 | tf_op jit(solution)/shard_map/ppermute | solution.py:176
  27.9 15.7 %collective-permute-start.14 = (bf16[128,1024]{1,0:T(8,128)(2,1)S(1)}, bf16[128,1024]{1,0:T(8,128)(2,1)S(1)}, u32[]{:S(2)}, u32[]{:S(2)}) collective-permute-start(bf16[128,1024]{1,0:T(8,128)(2,1)S(1)} %get-tuple-element.24.v4), channel_id=1, source_target_pairs={{0,4},{1,5},{2,6},{3,7},{4,8},{5,9},{6,10},{7,11},{8,12},{9,13},{1... | collective-permute-start | bytes 786440 | tf_op jit(solution)/shard_map/ppermute | solution.py:176
  31.4 23.5 %collective-permute-start.22 = (bf16[128,1024]{1,0:T(8,128)(2,1)S(1)}, bf16[128,1024]{1,0:T(8,128)(2,1)S(1)}, u32[]{:S(2)}, u32[]{:S(2)}) collective-permute-start(bf16[128,1024]{1,0:T(8,128)(2,1)S(1)} %get-tuple-element.26.v4), channel_id=1, source_target_pairs={{0,4},{1,5},{2,6},{3,7},{4,8},{5,9},{6,10},{7,11},{8,12},{9,13},{1... | collective-permute-start | bytes 786440 | tf_op jit(solution)/shard_map/ppermute | solution.py:176
  33.4 88.6 %copy-start = (bf16[128,4096]{1,0:T(8,128)(2,1)S(1)}, bf16[128,4096]{1,0:T(8,128)(2,1)}, u32[]{:S(2)}) copy-start(bf16[128,4096]{1,0:T(8,128)(2,1)} %pair_keys.7) | copy-start | bytes 3145732
  33.4 88.6 %copy-start.1 = (bf16[128,4096]{1,0:T(8,128)(2,1)S(1)}, bf16[128,4096]{1,0:T(8,128)(2,1)}, u32[]{:S(2)}) copy-start(bf16[128,4096]{1,0:T(8,128)(2,1)} %pair_values.7) | copy-start | bytes 3145732
  33.4 88.6 %copy-start.2 = (bf16[128,4096]{1,0:T(8,128)(2,1)S(1)}, bf16[128,4096]{1,0:T(8,128)(2,1)}, u32[]{:S(2)}) copy-start(bf16[128,4096]{1,0:T(8,128)(2,1)} %query.7) | copy-start | bytes 3145732
  33.4 32.7 %collective-permute-start.30 = (bf16[128,1024]{1,0:T(8,128)(2,1)S(1)}, bf16[128,1024]{1,0:T(8,128)(2,1)S(1)}, u32[]{:S(2)}, u32[]{:S(2)}) collective-permute-start(bf16[128,1024]{1,0:T(8,128)(2,1)S(1)} %get-tuple-element.25.v4), channel_id=1, source_target_pairs={{0,4},{1,5},{2,6},{3,7},{4,8},{5,9},{6,10},{7,11},{8,12},{9,13},{1... | collective-permute-start | bytes 786440 | tf_op jit(solution)/shard_map/ppermute | solution.py:176
  43.6 36.9 %collective-permute-start.10 = (bf16[128,1024]{1,0:T(8,128)(2,1)S(1)}, bf16[128,1024]{1,0:T(8,128)(2,1)S(1)}, u32[]{:S(2)}, u32[]{:S(2)}) collective-permute-start(bf16[128,1024]{1,0:T(8,128)(2,1)S(1)} %get-tuple-element.27.k4), channel_id=1, source_target_pairs={{0,4},{1,5},{2,6},{3,7},{4,8},{5,9},{6,10},{7,11},{8,12},{9,13},{1... | collective-permute-start | bytes 786440 | tf_op jit(solution)/shard_map/ppermute | solution.py:176
  54.9 31.6 %collective-permute-start.18 = (bf16[128,1024]{1,0:T(8,128)(2,1)S(1)}, bf16[128,1024]{1,0:T(8,128)(2,1)S(1)}, u32[]{:S(2)}, u32[]{:S(2)}) collective-permute-start(bf16[128,1024]{1,0:T(8,128)(2,1)S(1)} %get-tuple-element.29.k4), channel_id=1, source_target_pairs={{0,4},{1,5},{2,6},{3,7},{4,8},{5,9},{6,10},{7,11},{8,12},{9,13},{1... | collective-permute-start | bytes 786440 | tf_op jit(solution)/shard_map/ppermute | solution.py:176
  66.1 25.7 %collective-permute-start.26 = (bf16[128,1024]{1,0:T(8,128)(2,1)S(1)}, bf16[128,1024]{1,0:T(8,128)(2,1)S(1)}, u32[]{:S(2)}, u32[]{:S(2)}) collective-permute-start(bf16[128,1024]{1,0:T(8,128)(2,1)S(1)} %get-tuple-element.28.k4), channel_id=1, source_target_pairs={{0,4},{1,5},{2,6},{3,7},{4,8},{5,9},{6,10},{7,11},{8,12},{9,13},{1... | collective-permute-start | bytes 786440 | tf_op jit(solution)/shard_map/ppermute | solution.py:176
  75.9 16.0 %collective-permute-start.9 = (bf16[16,4096]{1,0:T(8,128)(2,1)S(1)}, bf16[16,4096]{1,0:T(8,128)(2,1)S(1)}, u32[]{:S(2)}, u32[]{:S(2)}) collective-permute-start(bf16[16,4096]{1,0:T(8,128)(2,1)S(1)} %slice.37), channel_id=1, source_target_pairs={{0,1},{1,2},{2,3},{3,4},{4,5},{5,6},{6,7},{7,8},{8,9},{9,10},{10,1... | collective-permute-start | bytes 393224 | tf_op jit(solution)/shard_map/ppermute | solution.py:214
  77.3 17.8 %collective-permute-start.1 = (bf16[128,1024]{1,0:T(8,128)(2,1)S(1)}, bf16[128,1024]{1,0:T(8,128)(2,1)S(1)}, u32[]{:S(2)}, u32[]{:S(2)}) collective-permute-start(bf16[128,1024]{1,0:T(8,128)(2,1)S(1)} %get-tuple-element.11), channel_id=1, source_target_pairs={{0,2},{1,3},{2,0},{3,1},{4,6},{5,7},{6,4},{7,5},{8,10},{9,11},{10,... | collective-permute-start | bytes 786440 | tf_op jit(solution)/shard_map/ppermute | solution.py:176
  80.6 17.6 %collective-permute-start.6 = (bf16[128,1024]{1,0:T(8,128)(2,1)S(1)}, bf16[128,1024]{1,0:T(8,128)(2,1)S(1)}, u32[]{:S(2)}, u32[]{:S(2)}) collective-permute-start(bf16[128,1024]{1,0:T(8,128)(2,1)S(1)} %get-tuple-element.8), channel_id=1, source_target_pairs={{0,1},{1,0},{2,3},{3,2},{4,5},{5,4},{6,7},{7,6},{8,9},{9,8},{10,11... | collective-permute-start | bytes 786440 | tf_op jit(solution)/shard_map/ppermute | solution.py:176
  86.4 12.1 %collective-permute-start.2 = (bf16[128,1024]{1,0:T(8,128)(2,1)S(1)}, bf16[128,1024]{1,0:T(8,128)(2,1)S(1)}, u32[]{:S(2)}, u32[]{:S(2)}) collective-permute-start(bf16[128,1024]{1,0:T(8,128)(2,1)S(1)} %get-tuple-element.10), channel_id=1, source_target_pairs={{0,1},{1,0},{2,3},{3,2},{4,5},{5,4},{6,7},{7,6},{8,9},{9,8},{10,11... | collective-permute-start | bytes 786440 | tf_op jit(solution)/shard_map/ppermute | solution.py:176
  91.8 6.7 %collective-permute-start.7 = (bf16[128,1024]{1,0:T(8,128)(2,1)S(1)}, bf16[128,1024]{1,0:T(8,128)(2,1)S(1)}, u32[]{:S(2)}, u32[]{:S(2)}) collective-permute-start(bf16[128,1024]{1,0:T(8,128)(2,1)S(1)} %collective-permute-done.5.v1), channel_id=1, source_target_pairs={{0,1},{1,0},{2,3},{3,2},{4,5},{5,4},{6,7},{7,6},{8,9},{9,8},{10,11... | collective-permute-start | bytes 786440 | tf_op jit(solution)/shard_map/ppermute | solution.py:176
  91.9 14.6 %collective-permute-start.15 = (bf16[128,1024]{1,0:T(8,128)(2,1)S(1)}, bf16[128,1024]{1,0:T(8,128)(2,1)S(1)}, u32[]{:S(2)}, u32[]{:S(2)}) collective-permute-start(bf16[128,1024]{1,0:T(8,128)(2,1)S(1)} %get-tuple-element.13), channel_id=1, source_target_pairs={{0,2},{1,3},{2,0},{3,1},{4,6},{5,7},{6,4},{7,5},{8,10},{9,11},{10,... | collective-permute-start | bytes 786440 | tf_op jit(solution)/shard_map/ppermute | solution.py:176
  95.0 15.7 %collective-permute-start.16 = (bf16[128,1024]{1,0:T(8,128)(2,1)S(1)}, bf16[128,1024]{1,0:T(8,128)(2,1)S(1)}, u32[]{:S(2)}, u32[]{:S(2)}) collective-permute-start(bf16[128,1024]{1,0:T(8,128)(2,1)S(1)} %get-tuple-element.12), channel_id=1, source_target_pairs={{0,1},{1,0},{2,3},{3,2},{4,5},{5,4},{6,7},{7,6},{8,9},{9,8},{10,11... | collective-permute-start | bytes 786440 | tf_op jit(solution)/shard_map/ppermute | solution.py:176
  98.2 19.6 %collective-permute-start.11 = (bf16[128,1024]{1,0:T(8,128)(2,1)S(1)}, bf16[128,1024]{1,0:T(8,128)(2,1)S(1)}, u32[]{:S(2)}, u32[]{:S(2)}) collective-permute-start(bf16[128,1024]{1,0:T(8,128)(2,1)S(1)} %get-tuple-element.15), channel_id=1, source_target_pairs={{0,2},{1,3},{2,0},{3,1},{4,6},{5,7},{6,4},{7,5},{8,10},{9,11},{10,... | collective-permute-start | bytes 786440 | tf_op jit(solution)/shard_map/ppermute | solution.py:176
  98.5 23.5 %collective-permute-start.12 = (bf16[128,1024]{1,0:T(8,128)(2,1)S(1)}, bf16[128,1024]{1,0:T(8,128)(2,1)S(1)}, u32[]{:S(2)}, u32[]{:S(2)}) collective-permute-start(bf16[128,1024]{1,0:T(8,128)(2,1)S(1)} %get-tuple-element.14), channel_id=1, source_target_pairs={{0,1},{1,0},{2,3},{3,2},{4,5},{5,4},{6,7},{7,6},{8,9},{9,8},{10,11... | collective-permute-start | bytes 786440 | tf_op jit(solution)/shard_map/ppermute | solution.py:176
  98.5 2.1 collective-permute-start.3
  100.6 35.2 %collective-permute-start.23 = (bf16[128,1024]{1,0:T(8,128)(2,1)S(1)}, bf16[128,1024]{1,0:T(8,128)(2,1)S(1)}, u32[]{:S(2)}, u32[]{:S(2)}) collective-permute-start(bf16[128,1024]{1,0:T(8,128)(2,1)S(1)} %get-tuple-element.30), channel_id=1, source_target_pairs={{0,2},{1,3},{2,0},{3,1},{4,6},{5,7},{6,4},{7,5},{8,10},{9,11},{10,... | collective-permute-start | bytes 786440 | tf_op jit(solution)/shard_map/ppermute | solution.py:176
  106.6 29.9 %collective-permute-start.24 = (bf16[128,1024]{1,0:T(8,128)(2,1)S(1)}, bf16[128,1024]{1,0:T(8,128)(2,1)S(1)}, u32[]{:S(2)}, u32[]{:S(2)}) collective-permute-start(bf16[128,1024]{1,0:T(8,128)(2,1)S(1)} %get-tuple-element.31), channel_id=1, source_target_pairs={{0,1},{1,0},{2,3},{3,2},{4,5},{5,4},{6,7},{7,6},{8,9},{9,8},{10,11... | collective-permute-start | bytes 786440 | tf_op jit(solution)/shard_map/ppermute | solution.py:176
  110.8 29.5 %collective-permute-start.19 = (bf16[128,1024]{1,0:T(8,128)(2,1)S(1)}, bf16[128,1024]{1,0:T(8,128)(2,1)S(1)}, u32[]{:S(2)}, u32[]{:S(2)}) collective-permute-start(bf16[128,1024]{1,0:T(8,128)(2,1)S(1)} %get-tuple-element.34), channel_id=1, source_target_pairs={{0,2},{1,3},{2,0},{3,1},{4,6},{5,7},{6,4},{7,5},{8,10},{9,11},{10,... | collective-permute-start | bytes 786440 | tf_op jit(solution)/shard_map/ppermute | solution.py:176
  117.8 24.9 %collective-permute-start.17 = (bf16[128,1024]{1,0:T(8,128)(2,1)S(1)}, bf16[128,1024]{1,0:T(8,128)(2,1)S(1)}, u32[]{:S(2)}, u32[]{:S(2)}) collective-permute-start(bf16[128,1024]{1,0:T(8,128)(2,1)S(1)} %collective-permute-done.15.v1), channel_id=1, source_target_pairs={{0,1},{1,0},{2,3},{3,2},{4,5},{5,4},{6,7},{7,6},{8,9},{9,8},{10,11... | collective-permute-start | bytes 786440 | tf_op jit(solution)/shard_map/ppermute | solution.py:176
  122.0 23.9 %collective-permute-start.13 = (bf16[128,1024]{1,0:T(8,128)(2,1)S(1)}, bf16[128,1024]{1,0:T(8,128)(2,1)S(1)}, u32[]{:S(2)}, u32[]{:S(2)}) collective-permute-start(bf16[128,1024]{1,0:T(8,128)(2,1)S(1)} %collective-permute-done.11.k1), channel_id=1, source_target_pairs={{0,1},{1,0},{2,3},{3,2},{4,5},{5,4},{6,7},{7,6},{8,9},{9,8},{10,11... | collective-permute-start | bytes 786440 | tf_op jit(solution)/shard_map/ppermute | solution.py:176
  135.8 24.0 %collective-permute-start.20 = (bf16[128,1024]{1,0:T(8,128)(2,1)S(1)}, bf16[128,1024]{1,0:T(8,128)(2,1)S(1)}, u32[]{:S(2)}, u32[]{:S(2)}) collective-permute-start(bf16[128,1024]{1,0:T(8,128)(2,1)S(1)} %get-tuple-element.35), channel_id=1, source_target_pairs={{0,1},{1,0},{2,3},{3,2},{4,5},{5,4},{6,7},{7,6},{8,9},{9,8},{10,11... | collective-permute-start | bytes 786440 | tf_op jit(solution)/shard_map/ppermute | solution.py:176
  136.4 23.9 %collective-permute-start.31 = (bf16[128,1024]{1,0:T(8,128)(2,1)S(1)}, bf16[128,1024]{1,0:T(8,128)(2,1)S(1)}, u32[]{:S(2)}, u32[]{:S(2)}) collective-permute-start(bf16[128,1024]{1,0:T(8,128)(2,1)S(1)} %get-tuple-element.32), channel_id=1, source_target_pairs={{0,2},{1,3},{2,0},{3,1},{4,6},{5,7},{6,4},{7,5},{8,10},{9,11},{10,... | collective-permute-start | bytes 786440 | tf_op jit(solution)/shard_map/ppermute | solution.py:176
  140.3 22.5 %collective-permute-start.27 = (bf16[128,1024]{1,0:T(8,128)(2,1)S(1)}, bf16[128,1024]{1,0:T(8,128)(2,1)S(1)}, u32[]{:S(2)}, u32[]{:S(2)}) collective-permute-start(bf16[128,1024]{1,0:T(8,128)(2,1)S(1)} %get-tuple-element.36), channel_id=1, source_target_pairs={{0,2},{1,3},{2,0},{3,1},{4,6},{5,7},{6,4},{7,5},{8,10},{9,11},{10,... | collective-permute-start | bytes 786440 | tf_op jit(solution)/shard_map/ppermute | solution.py:176
  142.7 23.3 %collective-permute-start.25 = (bf16[128,1024]{1,0:T(8,128)(2,1)S(1)}, bf16[128,1024]{1,0:T(8,128)(2,1)S(1)}, u32[]{:S(2)}, u32[]{:S(2)}) collective-permute-start(bf16[128,1024]{1,0:T(8,128)(2,1)S(1)} %collective-permute-done.23.v1), channel_id=1, source_target_pairs={{0,1},{1,0},{2,3},{3,2},{4,5},{5,4},{6,7},{7,6},{8,9},{9,8},{10,11... | collective-permute-start | bytes 786440 | tf_op jit(solution)/shard_map/ppermute | solution.py:176
  145.9 20.0 %collective-permute-start.21 = (bf16[128,1024]{1,0:T(8,128)(2,1)S(1)}, bf16[128,1024]{1,0:T(8,128)(2,1)S(1)}, u32[]{:S(2)}, u32[]{:S(2)}) collective-permute-start(bf16[128,1024]{1,0:T(8,128)(2,1)S(1)} %collective-permute-done.19.k1), channel_id=1, source_target_pairs={{0,1},{1,0},{2,3},{3,2},{4,5},{5,4},{6,7},{7,6},{8,9},{9,8},{10,11... | collective-permute-start | bytes 786440 | tf_op jit(solution)/shard_map/ppermute | solution.py:176
  159.8 20.1 %collective-permute-start.32 = (bf16[128,1024]{1,0:T(8,128)(2,1)S(1)}, bf16[128,1024]{1,0:T(8,128)(2,1)S(1)}, u32[]{:S(2)}, u32[]{:S(2)}) collective-permute-start(bf16[128,1024]{1,0:T(8,128)(2,1)S(1)} %get-tuple-element.33), channel_id=1, source_target_pairs={{0,1},{1,0},{2,3},{3,2},{4,5},{5,4},{6,7},{7,6},{8,9},{9,8},{10,11... | collective-permute-start | bytes 786440 | tf_op jit(solution)/shard_map/ppermute | solution.py:176
  160.3 19.6 %collective-permute-start.28 = (bf16[128,1024]{1,0:T(8,128)(2,1)S(1)}, bf16[128,1024]{1,0:T(8,128)(2,1)S(1)}, u32[]{:S(2)}, u32[]{:S(2)}) collective-permute-start(bf16[128,1024]{1,0:T(8,128)(2,1)S(1)} %get-tuple-element.37), channel_id=1, source_target_pairs={{0,1},{1,0},{2,3},{3,2},{4,5},{5,4},{6,7},{7,6},{8,9},{9,8},{10,11... | collective-permute-start | bytes 786440 | tf_op jit(solution)/shard_map/ppermute | solution.py:176
  162.7 17.2 %collective-permute-start.33 = (bf16[128,1024]{1,0:T(8,128)(2,1)S(1)}, bf16[128,1024]{1,0:T(8,128)(2,1)S(1)}, u32[]{:S(2)}, u32[]{:S(2)}) collective-permute-start(bf16[128,1024]{1,0:T(8,128)(2,1)S(1)} %collective-permute-done.31.v1), channel_id=1, source_target_pairs={{0,1},{1,0},{2,3},{3,2},{4,5},{5,4},{6,7},{7,6},{8,9},{9,8},{10,11... | collective-permute-start | bytes 786440 | tf_op jit(solution)/shard_map/ppermute | solution.py:176
  165.9 14.0 %collective-permute-start.29 = (bf16[128,1024]{1,0:T(8,128)(2,1)S(1)}, bf16[128,1024]{1,0:T(8,128)(2,1)S(1)}, u32[]{:S(2)}, u32[]{:S(2)}) collective-permute-start(bf16[128,1024]{1,0:T(8,128)(2,1)S(1)} %collective-permute-done.27.k1), channel_id=1, source_target_pairs={{0,1},{1,0},{2,3},{3,2},{4,5},{5,4},{6,7},{7,6},{8,9},{9,8},{10,11... | collective-permute-start | bytes 786440 | tf_op jit(solution)/shard_map/ppermute | solution.py:176
  193.8 19.4 %copy-start.8 = (f32[2048]{0:T(1024)S(1)}, f32[2048]{0:T(1024)}, u32[]{:S(2)}) copy-start(f32[2048]{0:T(1024)} %param.18) | copy-start | bytes 24580
  212.2 1.0 copy-start.5
  235.3 12.5 %copy-start.7 = (s32[128,4]{0,1:T(4,128)S(1)}, s32[128,4]{0,1:T(4,128)}, u32[]{:S(2)}) copy-start(s32[128,4]{0,1:T(4,128)} %param.22) | copy-start | bytes 6148
  235.3 12.7 %copy-start.9 = (f32[128,4]{0,1:T(4,128)S(1)}, f32[128,4]{0,1:T(4,128)}, u32[]{:S(2)}) copy-start(f32[128,4]{0,1:T(4,128)} %param.23) | copy-start | bytes 6148
  243.4 18.5 %all-to-all-start.1 = ((bf16[16,2,4,2048]{3,2,1,0:T(4,128)(2,1)}), bf16[16,2,4,2048]{3,2,1,0:T(4,128)(2,1)S(1)}, u32[]{:S(2)}, u32[]{:S(2)}) async-start(bf16[16,2,4,2048]{3,2,1,0:T(4,128)(2,1)} %bitcast.12), calls=%async_computation.1 | async-start | bytes 1048576 | tf_op jit(solution)/shard_map/all_to_all | solution.py:274
  264.5 7.9 %copy-start.6 = (f32[128,2048]{1,0:T(8,128)S(1)}, f32[128,2048]{1,0:T(8,128)}, u32[]{:S(2)}) copy-start(f32[128,2048]{1,0:T(8,128)} %copy-done.5) | copy-start | bytes 3145732
Sparse Core Ops, SparseCore 0:
  9.5 194.4 all-gather.1

commit v2 on v1

--- a/solution.py
+++ b/solution.py
@@ -133,12 +133,13 @@
     lax.fori_loop(0, heads // 2, pair, 0)
 
 
-def attention(query, key_blocks, value_blocks, key_tail, pair_keys, value_tail, pair_values,
+def attention(query, window, key_tail, pair_keys, value_tail, pair_values,
               chunk, width):
     length = query.shape[0]
-    blocks = len(key_blocks)
+    blocks = len(window)
     whole = pl.BlockSpec((length, width), lambda i: (0, chunk))
     sliced = pl.BlockSpec((length, width), lambda i: (0, 0))
+    lower = pl.BlockSpec((length, width), lambda i: (1, 0))
     tail = pl.BlockSpec((TAIL, width), lambda i: (0, chunk))
     rows = WIN_PAIRS * length
     keys = blocks * length
@@ -147,7 +148,7 @@
         attention_kernel,
         grid=(1,),
         out_shape=jax.ShapeDtypeStruct((length, width), jnp.bfloat16),
-        in_specs=[whole] + [sliced] * (2 * blocks) + [tail, whole, tail, whole],
+        in_specs=[whole] + [sliced] * blocks + [lower] * blocks + [tail, whole, tail, whole],
         out_specs=sliced,
         scratch_shapes=[
             pltpu.VMEM((keys, 2 * HEAD_DIM), jnp.bfloat16),
@@ -168,24 +169,22 @@
             bytes_accessed=(2 * blocks + 4) * length * width * 2,
             transcendentals=heads * rows * keys,
         ),
-    )(query, *key_blocks, *value_blocks, key_tail, pair_keys, value_tail, pair_values)
-
-
-def spread_blocks(keys, values, devices, device):
-    def move(arrays, pairs):
-        return lax.ppermute(arrays, "wide", pairs)
-
-    own = (keys, values)
-    far = move(own, [(i, i + 4) for i in range(devices - 4)])
-    low = lax.rem(device, 4) < 2
-    sent = tuple(jnp.where(low, a, b) for a, b in zip(own, far))
-    middle = move(sent, [(i, i ^ 2) for i in range(devices)])
-    even = lax.rem(device, 2) == 0
-    sent = tuple(jnp.where(even, a, b) for a, b in zip(own, far))
+    )(query, *window, *window, key_tail, pair_keys, value_tail, pair_values)
+
+
+def spread_blocks(own, devices, device, after):
+    far = lax.ppermute(own, "wide", [(i, i + 4) for i in range(devices - 4)])
+    sent = jnp.where(lax.rem(device, 4) < 2, own, far)
+    middle = lax.ppermute(sent, "wide", [(i, i ^ 2) for i in range(devices)])
+    sent = jnp.where(lax.rem(device, 2) == 0, own, far)
+    if after is not None:
+        sent, moved, after = lax.optimization_barrier((sent, middle, after))
+    else:
+        moved = middle
     swap = [(i, i ^ 1) for i in range(devices)]
-    first = move(sent, swap)
-    second = move(middle, swap)
-    return tuple(zip(far, middle, first, second, own))
+    first = lax.ppermute(sent, "wide", swap)
+    second = lax.ppermute(moved, "wide", swap)
+    return (far, moved, first, second, own), after
 
 
 def on_device(
@@ -220,11 +219,13 @@
     pieces = []
     for chunk in range(chunks):
         cols = slice(chunk * chunk_width, (chunk + 1) * chunk_width)
-        key_blocks, value_blocks = spread_blocks(
-            first_keys[:, cols], first_values[:, cols], devices, device
-        )
+        own = jnp.concatenate([first_keys[:, cols], first_values[:, cols]], axis=0)
+        after = pieces[chunk - 2] if chunk >= 2 else None
+        window, after = spread_blocks(own, devices, device, after)
+        if after is not None:
+            pieces[chunk - 2] = after
         pieces.append(
-            attention(queries, key_blocks, value_blocks, key_tail, second_keys,
+            attention(queries, window, key_tail, second_keys,
                       value_tail, second_values, chunk, chunk_width)
         )
     attended = jnp.concatenate(pieces, axis=1)

time: 281 us -> 278 us (0.989)
  starting transfers between devices: 88.5 us -> 43.5 us
  waiting for transfers between devices: 61.9 us -> 95.8 us
  local copies, waits for them, and re-layouts: 14.7 us -> 18.9 us
    ppermute x32 -> x16, starting transfers between devices: 81.9 us -> 33.9 us  [the longest x4 15.8 us: spread_blocks(): far = lax.ppermute(own, 'wide', [(i, i + 4) for i in range(devices - 4)])]
    ppermute x32 -> x16, waiting for transfers between devices: 37.3 us -> 59.8 us  [the longest x4 40.2 us: spread_blocks(): far = lax.ppermute(own, 'wide', [(i, i + 4) for i in range(devices - 4)])]
    all_gather x1, waiting for transfers between devices: 10.2 us -> 21.7 us  [on_device(): full_weight = lax.all_gather(out_weight, 'wide', axis=0, tiled=True)]
    ppermute x2, starting transfers between devices: 2.59 us -> 5.44 us  [on_device(): lax.ppermute((second_keys[length - TAIL:], second_values[length - TAIL:])...]
  transfers between devices with their start and end apart: 36 -> 20, of which waited for: 12 -> 7; matrix products, arithmetic and copies ran while one was open for 3% -> 6% of each run, Pallas kernels for 20% -> 20%
where the time goes in v2:
time: 278 us; the launch traced here: 277 us
  waiting for transfers between devices  95.8 us (34%)
  Pallas kernels  55.6 us (20%)
  starting transfers between devices  43.5 us (16%)
  matrix products  19.3 us (7%)
  local copies, waits for them, and re-layouts  18.9 us (7%)
  blocking collectives  18.4 us (7%)
  between operations  14 us (5%)
  other arithmetic  11.7 us (4%)
    pallas_call x4, Pallas kernels, attention(): pl.pallas_call(attention_kernel, grid=(1,), out_shape=jax.ShapeDtypeStruc...  55.6 us
    ppermute x4, waiting for transfers between devices, spread_blocks(): far = lax.ppermute(own, 'wide', [(i, i + 4) for i in range(devices - 4)])  40.2 us
    all_gather x1, waiting for transfers between devices, on_device(): full_weight = lax.all_gather(out_weight, 'wide', axis=0, tiled=True)  21.7 us
    ppermute x4, waiting for transfers between devices, spread_blocks(): middle = lax.ppermute(sent, 'wide', [(i, i ^ 2) for i in range(devices)])  19.6 us
    all_to_all x1, blocking collectives, on_device(): lax.all_to_all(outgoing, 'wide', split_axis=0, concat_axis=0, tiled=True)  18.4 us
    ppermute x4, starting transfers between devices, spread_blocks(): far = lax.ppermute(own, 'wide', [(i, i + 4) for i in range(devices - 4)])  15.8 us
    all_to_all x1, waiting for transfers between devices, on_device(): lax.all_to_all(finished, 'wide', split_axis=0, concat_axis=0, tiled=True)  13.6 us
    ppermute x4, starting transfers between devices, spread_blocks(): middle = lax.ppermute(sent, 'wide', [(i, i ^ 2) for i in range(devices)])  12.6 us
  transfers between devices with their start and end apart: 20, of which 7 were waited for; matrix products, arithmetic and copies ran while one was open for 6% of the time, Pallas kernels for 20%

profile of v2, /device:TPU:0, one launch (start us, length us, event | category | flops | bytes accessed | tf_op | source)
XLA Modules:
  0.0 277.2 jit_solution(9657338612319642659)
XLA Ops:
  6.5 0.7 all-gather.2.cloned.1.call-update
  7.3 2.5 fusion.21
  9.8 0.7 copy-done.12
  10.6 5.0 %collective-permute-start.2 = (bf16[256,1024]{1,0:T(8,128)(2,1)S(1)}, bf16[256,1024]{1,0:T(8,128)(2,1)S(1)}, u32[]{:S(2)}, u32[]{:S(2)}) collective-permute-start(bf16[256,1024]{1,0:T(8,128)(2,1)S(1)} %pad_maximum_fusion.1.k4.v4), channel_id=1, source_target_pairs={{0,4},{1,5},{2,6},{3,7},{4,8},{5,9},{6,10},{7,11},{8,12},{9,13},{1... | collective-permute-start | bytes 1572872 | tf_op jit(solution)/shard_map/ppermute | solution.py:176
  15.5 1.6 slice.38
  17.1 2.1 collective-permute-start.6
  19.2 1.6 slice.39
  20.8 3.3 %collective-permute-start.7 = (bf16[16,4096]{1,0:T(8,128)(2,1)}, bf16[16,4096]{1,0:T(8,128)(2,1)S(1)}, u32[]{:S(2)}, u32[]{:S(2)}) collective-permute-start(bf16[16,4096]{1,0:T(8,128)(2,1)} %slice.39), channel_id=1, source_target_pairs={{0,1},{1,2},{2,3},{3,4},{4,5},{5,6},{6,7},{7,8},{8,9},{9,10},{10,1... | collective-permute-start | bytes 393224 | tf_op jit(solution)/shard_map/ppermute | solution.py:213
  24.2 3.5 %collective-permute-start = (bf16[256,1024]{1,0:T(8,128)(2,1)S(1)}, bf16[256,1024]{1,0:T(8,128)(2,1)S(1)}, u32[]{:S(2)}, u32[]{:S(2)}) collective-permute-start(bf16[256,1024]{1,0:T(8,128)(2,1)S(1)} %pad_maximum_fusion.k4.v4), channel_id=1, source_target_pairs={{0,4},{1,5},{2,6},{3,7},{4,8},{5,9},{6,10},{7,11},{8,12},{9,13},{1... | collective-permute-start | bytes 1572872 | tf_op jit(solution)/shard_map/ppermute | solution.py:176
  27.8 3.5 %collective-permute-start.10 = (bf16[256,1024]{1,0:T(8,128)(2,1)S(1)}, bf16[256,1024]{1,0:T(8,128)(2,1)S(1)}, u32[]{:S(2)}, u32[]{:S(2)}) collective-permute-start(bf16[256,1024]{1,0:T(8,128)(2,1)S(1)} %pad_maximum_fusion.3.k4.v4), channel_id=1, source_target_pairs={{0,4},{1,5},{2,6},{3,7},{4,8},{5,9},{6,10},{7,11},{8,12},{9,13},{1... | collective-permute-start | bytes 1572872 | tf_op jit(solution)/shard_map/ppermute | solution.py:176
  31.3 0.7 copy.37
  32.0 0.9 reshape.118
  33.2 0.7 reduce_sum.32
  33.9 0.9 copy.38
  34.9 0.6 compare_and_fusion
  35.5 0.9 slice_reduce_fusion
  36.4 1.0 pad_maximum_fusion.2.k4.v4
  37.4 3.9 %collective-permute-start.8 = (bf16[256,1024]{1,0:T(8,128)(2,1)S(1)}, bf16[256,1024]{1,0:T(8,128)(2,1)S(1)}, u32[]{:S(2)}, u32[]{:S(2)}) collective-permute-start(bf16[256,1024]{1,0:T(8,128)(2,1)S(1)} %pad_maximum_fusion.2.k4.v4), channel_id=1, source_target_pairs={{0,4},{1,5},{2,6},{3,7},{4,8},{5,9},{6,10},{7,11},{8,12},{9,13},{1... | collective-permute-start | bytes 1572872 | tf_op jit(solution)/shard_map/ppermute | solution.py:176
  41.3 1.3 broadcast_select_fusion.6
  42.6 1.5 collective-permute-start.3
  44.1 34.6 %collective-permute-done.10.k0.v0 = bf16[256,1024]{1,0:T(8,128)(2,1)S(1)} collective-permute-done((bf16[256,1024]{1,0:T(8,128)(2,1)S(1)}, bf16[256,1024]{1,0:T(8,128)(2,1)S(1)}, u32[]{:S(2)}, u32[]{:S(2)}) %collective-permute-start.10) | collective-permute-done | bytes 524320 | tf_op jit(solution)/shard_map/ppermute | solution.py:176
  78.8 1.3 broadcast_select_fusion.4
  80.1 8.1 %collective-permute-start.11 = (bf16[256,1024]{1,0:T(8,128)(2,1)S(1)}, bf16[256,1024]{1,0:T(8,128)(2,1)S(1)}, u32[]{:S(2)}, u32[]{:S(2)}) collective-permute-start(bf16[256,1024]{1,0:T(8,128)(2,1)S(1)} %get-tuple-element.33), channel_id=1, source_target_pairs={{0,2},{1,3},{2,0},{3,1},{4,6},{5,7},{6,4},{7,5},{8,10},{9,11},{10,... | collective-permute-start | bytes 1572872 | tf_op jit(solution)/shard_map/ppermute | solution.py:178
  88.5 5.6 %collective-permute-done.8.k0.v0 = bf16[256,1024]{1,0:T(8,128)(2,1)S(1)} collective-permute-done((bf16[256,1024]{1,0:T(8,128)(2,1)S(1)}, bf16[256,1024]{1,0:T(8,128)(2,1)S(1)}, u32[]{:S(2)}, u32[]{:S(2)}) %collective-permute-start.8) | collective-permute-done | bytes 524320 | tf_op jit(solution)/shard_map/ppermute | solution.py:176
  94.1 2.7 collective-permute-start.1
  97.0 4.5 %collective-permute-start.12 = (bf16[256,1024]{1,0:T(8,128)(2,1)S(1)}, bf16[256,1024]{1,0:T(8,128)(2,1)S(1)}, u32[]{:S(2)}, u32[]{:S(2)}) collective-permute-start(bf16[256,1024]{1,0:T(8,128)(2,1)S(1)} %get-tuple-element.32), channel_id=1, source_target_pairs={{0,1},{1,0},{2,3},{3,2},{4,5},{5,4},{6,7},{7,6},{8,9},{9,8},{10,11... | collective-permute-start | bytes 1572872 | tf_op jit(solution)/shard_map/ppermute | solution.py:185
  101.8 3.9 %collective-permute-done.11.k1.v1 = bf16[256,1024]{1,0:T(8,128)(2,1)S(1)} collective-permute-done((bf16[256,1024]{1,0:T(8,128)(2,1)S(1)}, bf16[256,1024]{1,0:T(8,128)(2,1)S(1)}, u32[]{:S(2)}, u32[]{:S(2)}) %collective-permute-start.11) | collective-permute-done | bytes 524320 | tf_op jit(solution)/shard_map/ppermute | solution.py:178
  105.8 14.0 %shard_map.118 = bf16[128,1024]{1,0:T(8,128)(2,1)S(1)} custom-call(bf16[128,4096]{1,0:T(8,128)(2,1)S(1)} %copy-done.2, bf16[256,1024]{1,0:T(8,128)(2,1)S(1)} %collective-permute-done.2.k0.v0, bf16[256,1024]{1,0:T(8,128)(2,1)S(1)} %collective-permute-done.3.k1.v1, bf16[256,1024]{1,0:T(8,128)(2,1)S(1)} %collective-permute-done.4.k2.v2, ...), custom_call_target="tpu_custom_call" | custom-call | flops 8053063680 | bytes 3670016 | tf_op jit(solution)/shard_map/pallas_call | solution.py:147
  119.8 8.4 %collective-permute-done.1.k1.v1 = bf16[256,1024]{1,0:T(8,128)(2,1)S(1)} collective-permute-done((bf16[256,1024]{1,0:T(8,128)(2,1)S(1)}, bf16[256,1024]{1,0:T(8,128)(2,1)S(1)}, u32[]{:S(2)}, u32[]{:S(2)}) %collective-permute-start.1) | collective-permute-done | bytes 524320 | tf_op jit(solution)/shard_map/ppermute | solution.py:178
  128.2 0.5 collective-permute-start.15
  128.7 13.8 %shard_map.119 = bf16[128,1024]{1,0:T(8,128)(2,1)S(1)} custom-call(bf16[128,4096]{1,0:T(8,128)(2,1)S(1)} %copy-done.2, bf16[256,1024]{1,0:T(8,128)(2,1)S(1)} %collective-permute-done.10.k0.v0, bf16[256,1024]{1,0:T(8,128)(2,1)S(1)} %collective-permute-done.11.k1.v1, bf16[256,1024]{1,0:T(8,128)(2,1)S(1)} %collective-permute-done.12.k2.v2, ...), custom_call_target="tpu_custom_call" | custom-call | flops 8053063680 | bytes 3670016 | tf_op jit(solution)/shard_map/pallas_call | solution.py:147
  142.5 7.2 %collective-permute-done.9.k1.v1 = bf16[256,1024]{1,0:T(8,128)(2,1)S(1)} collective-permute-done((bf16[256,1024]{1,0:T(8,128)(2,1)S(1)}, bf16[256,1024]{1,0:T(8,128)(2,1)S(1)}, u32[]{:S(2)}, u32[]{:S(2)}) %collective-permute-start.9) | collective-permute-done | bytes 524320 | tf_op jit(solution)/shard_map/ppermute | solution.py:178
  149.7 0.5 collective-permute-start.17
  150.2 14.0 %shard_map.120 = bf16[128,1024]{1,0:T(8,128)(2,1)S(1)} custom-call(bf16[128,4096]{1,0:T(8,128)(2,1)S(1)} %copy-done.2, bf16[256,1024]{1,0:T(8,128)(2,1)S(1)} %collective-permute-done.k0.v0, bf16[256,1024]{1,0:T(8,128)(2,1)S(1)} %collective-permute-done.1.k1.v1, bf16[256,1024]{1,0:T(8,128)(2,1)S(1)} %collective-permute-done.14.k2.v2, ...), custom_call_target="tpu_custom_call" | custom-call | flops 8053063680 | bytes 3670016 | tf_op jit(solution)/shard_map/pallas_call | solution.py:147
  164.3 13.8 %shard_map.121 = bf16[128,1024]{1,0:T(8,128)(2,1)S(1)} custom-call(bf16[128,4096]{1,0:T(8,128)(2,1)S(1)} %copy-done.2, bf16[256,1024]{1,0:T(8,128)(2,1)S(1)} %collective-permute-done.8.k0.v0, bf16[256,1024]{1,0:T(8,128)(2,1)S(1)} %collective-permute-done.9.k1.v1, bf16[256,1024]{1,0:T(8,128)(2,1)S(1)} %collective-permute-done.16.k2.v2, ...), custom_call_target="tpu_custom_call" | custom-call | flops 8053063680 | bytes 3670016 | tf_op jit(solution)/shard_map/pallas_call | solution.py:147
  178.1 21.7 %all-gather.2.cloned.1.call-done = bf16[4096,2048]{1,0:T(8,128)(2,1)} async-done(((bf16[256,2048]{1,0:T(8,128)(2,1)}), bf16[4096,2048]{1,0:T(8,128)(2,1)}) %all-gather.2.cloned.1.call-update) | async-done | bytes 16777232 | tf_op jit(solution)/shard_map/all_gather | solution.py:212
  199.8 8.2 %multiply_reduce_fusion.1 = (f32[128]{0:T(128)S(1)}, f32[128,2048]{1,0:T(8,128)S(1)}) fusion(bf16[4096,2048]{1,0:T(8,128)(2,1)} %all-gather.2.cloned.1.call-done, bf16[128,1024]{1,0:T(8,128)(2,1)S(1)} %shard_map.121, bf16[128,1024]{1,0:T(8,128)(2,1)S(1)} %shard_map.120, bf16[128,1024]{1,0:T(8,128)(2,1)S(1)} %shard_map.119, bf16[128,1024]{1,0:T(8,128)(2,1)S(1)} %shard_map.118), kind=kOutput, calls=%fused_computation.17 | convolution fusion | flops 2152726528 | bytes 18874880 | tf_op jit(solution)/shard_map/dot_general | solution.py:233
  208.0 1.0 copy-done.3
  209.6 18.4 %all_to_all.10 = bf16[16,2,4,2048]{3,2,1,0:T(4,128)(2,1)S(1)} all-to-all(bf16[16,2,4,2048]{3,2,1,0:T(4,128)(2,1)S(1)} %reshape.119), channel_id=1, replica_groups=mesh['groups'=2,'wide'=16] {'wide'}, dimensions={0} | all-to-all | bytes 1048576 | tf_op jit(solution)/shard_map/all_to_all | solution.py:261
  228.3 3.9 %fusion.23 = f32[2,64,768]{2,1,0:T(8,128)S(1)} fusion(bf16[2,64,2048]{2,1,0:T(8,128)(2,1)S(1)} %reshape.120, bf16[2,2048,768]{2,1,0:T(8,128)(2,1)} %param.19), kind=kOutput, calls=%fused_computation.59 | convolution fusion | flops 402653184 | bytes 7208960 | tf_op jit(solution)/shard_map/erd,edf->erf/dot_general | solution.py:266
  232.2 6.8 %convolution_convert_fusion = bf16[2,64,2048]{2,1,0:T(8,128)(2,1)S(1)} fusion(bf16[2,768,2048]{2,1,0:T(8,128)(2,1)} %param.21, bf16[2,64,2048]{2,1,0:T(8,128)(2,1)S(1)} %reshape.120, bf16[2,2048,768]{2,1,0:T(8,128)(2,1)} %param.20, f32[2,64,768]{2,1,0:T(8,128)S(1)} %fusion.23), kind=kOutput, calls=%fused_computation.2 | convolution fusion | flops 806158336 | bytes 14024704 | tf_op jit(solution)/shard_map/erf,efd->erd/dot_general | solution.py:271
  239.3 1.0 copy.46
  240.3 4.1 %all-to-all-start.1 = ((bf16[16,2,4,2048]{3,2,1,0:T(4,128)(2,1)}), bf16[16,2,4,2048]{3,2,1,0:T(4,128)(2,1)S(1)}, u32[]{:S(2)}, u32[]{:S(2)}) async-start(bf16[16,2,4,2048]{3,2,1,0:T(4,128)(2,1)} %bitcast.12), calls=%async_computation.1 | async-start | bytes 1048576 | tf_op jit(solution)/shard_map/all_to_all | solution.py:275
  245.3 13.6 %all-to-all-done.1 = bf16[16,2,4,2048]{3,2,1,0:T(4,128)(2,1)S(1)} async-done(((bf16[16,2,4,2048]{3,2,1,0:T(4,128)(2,1)}), bf16[16,2,4,2048]{3,2,1,0:T(4,128)(2,1)S(1)}, u32[]{:S(2)}, u32[]{:S(2)}) %all-to-all-start.1) | async-done | bytes 524320 | tf_op jit(solution)/shard_map/all_to_all | solution.py:275
  259.0 2.5 gather_fusion
  261.5 2.2 gather.7
  263.7 5.6 %multiply_reduce_fusion = f32[128,2048]{1,0:T(8,128)S(1)} fusion(f32[128,4]{1,0:T(8,128)S(1)} %copy.44, bf16[128,4,2048]{2,1,0:T(4,128)(2,1)} %gather.7, pred[128,4]{1,0:T(8,128)(4,1)S(1)} %copy.39), kind=kLoop, calls=%fused_computation.1 | loop fusion | flops 3932160 | bytes 3148288 | tf_op jit(solution)/shard_map/reduce_sum | solution.py:280
  269.4 0.9 add_convert_fusion
  (87 shorter events, 3.4 us)
Async XLA Ops:
  6.5 193.2 %all-gather.2.cloned.1.call-start = ((), (), s32[]{:S(2)}) async-start(), calls=%async_computation.2 | async-start | bytes 17825792 | tf_op jit(solution)/shard_map/all_gather | solution.py:212
  7.3 24.0 %copy-start.14 = (s32[128,4]{0,1:T(4,128)S(1)}, s32[128,4]{0,1:T(4,128)}, u32[]{:S(2)}) copy-start(s32[128,4]{0,1:T(4,128)} %param.22) | copy-start | bytes 6148
  9.8 0.7 copy-start.12
  9.8 0.8 copy-start.13
  9.8 14.4 %copy-start.6 = (bf16[128,1024]{1,0:T(8,128)(2,1)}, bf16[128,1024]{1,0:T(8,128)(2,1)S(1)}, u32[]{:S(2)}) copy-start(bf16[128,1024]{1,0:T(8,128)(2,1)S(1)} %get-tuple-element.23) | copy-start | bytes 786436
  9.8 14.4 %copy-start.8 = (bf16[128,1024]{1,0:T(8,128)(2,1)}, bf16[128,1024]{1,0:T(8,128)(2,1)S(1)}, u32[]{:S(2)}) copy-start(bf16[128,1024]{1,0:T(8,128)(2,1)S(1)} %get-tuple-element.40) | copy-start | bytes 786436
  9.8 17.9 %copy-start.10 = (bf16[128,1024]{1,0:T(8,128)(2,1)}, bf16[128,1024]{1,0:T(8,128)(2,1)S(1)}, u32[]{:S(2)}) copy-start(bf16[128,1024]{1,0:T(8,128)(2,1)S(1)} %get-tuple-element.24) | copy-start | bytes 786436
  9.8 17.9 %copy-start.11 = (bf16[128,1024]{1,0:T(8,128)(2,1)}, bf16[128,1024]{1,0:T(8,128)(2,1)S(1)}, u32[]{:S(2)}) copy-start(bf16[128,1024]{1,0:T(8,128)(2,1)S(1)} %get-tuple-element.39) | copy-start | bytes 786436
  10.6 26.8 %collective-permute-start.2 = (bf16[256,1024]{1,0:T(8,128)(2,1)S(1)}, bf16[256,1024]{1,0:T(8,128)(2,1)S(1)}, u32[]{:S(2)}, u32[]{:S(2)}) collective-permute-start(bf16[256,1024]{1,0:T(8,128)(2,1)S(1)} %pad_maximum_fusion.1.k4.v4), channel_id=1, source_target_pairs={{0,4},{1,5},{2,6},{3,7},{4,8},{5,9},{6,10},{7,11},{8,12},{9,13},{1... | collective-permute-start | bytes 1572872 | tf_op jit(solution)/shard_map/ppermute | solution.py:176
  17.1 25.5 %collective-permute-start.6 = (bf16[16,4096]{1,0:T(8,128)(2,1)}, bf16[16,4096]{1,0:T(8,128)(2,1)}, u32[]{:S(2)}, u32[]{:S(2)}) collective-permute-start(bf16[16,4096]{1,0:T(8,128)(2,1)} %slice.38), channel_id=1, source_target_pairs={{0,1},{1,2},{2,3},{3,4},{4,5},{5,6},{6,7},{7,8},{8,9},{9,10},{10,1... | collective-permute-start | bytes 393224 | tf_op jit(solution)/shard_map/ppermute | solution.py:213
  20.8 76.2 %collective-permute-start.7 = (bf16[16,4096]{1,0:T(8,128)(2,1)}, bf16[16,4096]{1,0:T(8,128)(2,1)S(1)}, u32[]{:S(2)}, u32[]{:S(2)}) collective-permute-start(bf16[16,4096]{1,0:T(8,128)(2,1)} %slice.39), channel_id=1, source_target_pairs={{0,1},{1,2},{2,3},{3,4},{4,5},{5,6},{6,7},{7,8},{8,9},{9,10},{10,1... | collective-permute-start | bytes 393224 | tf_op jit(solution)/shard_map/ppermute | solution.py:213
  24.2 55.9 %collective-permute-start = (bf16[256,1024]{1,0:T(8,128)(2,1)S(1)}, bf16[256,1024]{1,0:T(8,128)(2,1)S(1)}, u32[]{:S(2)}, u32[]{:S(2)}) collective-permute-start(bf16[256,1024]{1,0:T(8,128)(2,1)S(1)} %pad_maximum_fusion.k4.v4), channel_id=1, source_target_pairs={{0,4},{1,5},{2,6},{3,7},{4,8},{5,9},{6,10},{7,11},{8,12},{9,13},{1... | collective-permute-start | bytes 1572872 | tf_op jit(solution)/shard_map/ppermute | solution.py:176
  27.8 51.0 %collective-permute-start.10 = (bf16[256,1024]{1,0:T(8,128)(2,1)S(1)}, bf16[256,1024]{1,0:T(8,128)(2,1)S(1)}, u32[]{:S(2)}, u32[]{:S(2)}) collective-permute-start(bf16[256,1024]{1,0:T(8,128)(2,1)S(1)} %pad_maximum_fusion.3.k4.v4), channel_id=1, source_target_pairs={{0,4},{1,5},{2,6},{3,7},{4,8},{5,9},{6,10},{7,11},{8,12},{9,13},{1... | collective-permute-start | bytes 1572872 | tf_op jit(solution)/shard_map/ppermute | solution.py:176
  33.2 2.3 copy-start.16
  34.8 53.4 %copy-start.7 = (bf16[128,1024]{1,0:T(8,128)(2,1)S(1)}, bf16[128,1024]{1,0:T(8,128)(2,1)}, u32[]{:S(2)}) copy-start(bf16[128,1024]{1,0:T(8,128)(2,1)} %copy-done.6) | copy-start | bytes 786436
  34.8 53.4 %copy-start.9 = (bf16[128,1024]{1,0:T(8,128)(2,1)S(1)}, bf16[128,1024]{1,0:T(8,128)(2,1)}, u32[]{:S(2)}) copy-start(bf16[128,1024]{1,0:T(8,128)(2,1)} %copy-done.8) | copy-start | bytes 786436
  34.8 61.9 %copy-start.5 = (bf16[128,1024]{1,0:T(8,128)(2,1)S(1)}, bf16[128,1024]{1,0:T(8,128)(2,1)}, u32[]{:S(2)}) copy-start(bf16[128,1024]{1,0:T(8,128)(2,1)} %get-tuple-element.38) | copy-start | bytes 786436
  37.4 68.4 %copy-start = (bf16[128,4096]{1,0:T(8,128)(2,1)S(1)}, bf16[128,4096]{1,0:T(8,128)(2,1)}, u32[]{:S(2)}) copy-start(bf16[128,4096]{1,0:T(8,128)(2,1)} %pair_keys.7) | copy-start | bytes 3145732
  37.4 68.4 %copy-start.1 = (bf16[128,4096]{1,0:T(8,128)(2,1)S(1)}, bf16[128,4096]{1,0:T(8,128)(2,1)}, u32[]{:S(2)}) copy-start(bf16[128,4096]{1,0:T(8,128)(2,1)} %pair_values.7) | copy-start | bytes 3145732
  37.4 68.4 %copy-start.2 = (bf16[128,4096]{1,0:T(8,128)(2,1)S(1)}, bf16[128,4096]{1,0:T(8,128)(2,1)}, u32[]{:S(2)}) copy-start(bf16[128,4096]{1,0:T(8,128)(2,1)} %query.7) | copy-start | bytes 3145732
  37.4 56.7 %collective-permute-start.8 = (bf16[256,1024]{1,0:T(8,128)(2,1)S(1)}, bf16[256,1024]{1,0:T(8,128)(2,1)S(1)}, u32[]{:S(2)}, u32[]{:S(2)}) collective-permute-start(bf16[256,1024]{1,0:T(8,128)(2,1)S(1)} %pad_maximum_fusion.2.k4.v4), channel_id=1, source_target_pairs={{0,4},{1,5},{2,6},{3,7},{4,8},{5,9},{6,10},{7,11},{8,12},{9,13},{1... | collective-permute-start | bytes 1572872 | tf_op jit(solution)/shard_map/ppermute | solution.py:176
  42.6 45.6 %collective-permute-start.3 = (bf16[256,1024]{1,0:T(8,128)(2,1)S(1)}, bf16[256,1024]{1,0:T(8,128)(2,1)S(1)}, u32[]{:S(2)}, u32[]{:S(2)}) collective-permute-start(bf16[256,1024]{1,0:T(8,128)(2,1)S(1)} %get-tuple-element.21), channel_id=1, source_target_pairs={{0,2},{1,3},{2,0},{3,1},{4,6},{5,7},{6,4},{7,5},{8,10},{9,11},{10,... | collective-permute-start | bytes 1572872 | tf_op jit(solution)/shard_map/ppermute | solution.py:178
  78.8 22.8 %collective-permute-start.4 = (bf16[256,1024]{1,0:T(8,128)(2,1)S(1)}, bf16[256,1024]{1,0:T(8,128)(2,1)S(1)}, u32[]{:S(2)}, u32[]{:S(2)}) collective-permute-start(bf16[256,1024]{1,0:T(8,128)(2,1)S(1)} %get-tuple-element.20), channel_id=1, source_target_pairs={{0,1},{1,0},{2,3},{3,2},{4,5},{5,4},{6,7},{7,6},{8,9},{9,8},{10,11... | collective-permute-start | bytes 1572872 | tf_op jit(solution)/shard_map/ppermute | solution.py:185
  80.1 25.7 %collective-permute-start.11 = (bf16[256,1024]{1,0:T(8,128)(2,1)S(1)}, bf16[256,1024]{1,0:T(8,128)(2,1)S(1)}, u32[]{:S(2)}, u32[]{:S(2)}) collective-permute-start(bf16[256,1024]{1,0:T(8,128)(2,1)S(1)} %get-tuple-element.33), channel_id=1, source_target_pairs={{0,2},{1,3},{2,0},{3,1},{4,6},{5,7},{6,4},{7,5},{8,10},{9,11},{10,... | collective-permute-start | bytes 1572872 | tf_op jit(solution)/shard_map/ppermute | solution.py:178
  88.2 17.5 %collective-permute-start.5 = (bf16[256,1024]{1,0:T(8,128)(2,1)S(1)}, bf16[256,1024]{1,0:T(8,128)(2,1)S(1)}, u32[]{:S(2)}, u32[]{:S(2)}) collective-permute-start(bf16[256,1024]{1,0:T(8,128)(2,1)S(1)} %collective-permute-done.3.k1.v1), channel_id=1, source_target_pairs={{0,1},{1,0},{2,3},{3,2},{4,5},{5,4},{6,7},{7,6},{8,9},{9,8},{10,11... | collective-permute-start | bytes 1572872 | tf_op jit(solution)/shard_map/ppermute | solution.py:186
  94.1 34.1 %collective-permute-start.1 = (bf16[256,1024]{1,0:T(8,128)(2,1)S(1)}, bf16[256,1024]{1,0:T(8,128)(2,1)S(1)}, u32[]{:S(2)}, u32[]{:S(2)}) collective-permute-start(bf16[256,1024]{1,0:T(8,128)(2,1)S(1)} %get-tuple-element.30), channel_id=1, source_target_pairs={{0,2},{1,3},{2,0},{3,1},{4,6},{5,7},{6,4},{7,5},{8,10},{9,11},{10,... | collective-permute-start | bytes 1572872 | tf_op jit(solution)/shard_map/ppermute | solution.py:178
  97.0 31.7 %collective-permute-start.12 = (bf16[256,1024]{1,0:T(8,128)(2,1)S(1)}, bf16[256,1024]{1,0:T(8,128)(2,1)S(1)}, u32[]{:S(2)}, u32[]{:S(2)}) collective-permute-start(bf16[256,1024]{1,0:T(8,128)(2,1)S(1)} %get-tuple-element.32), channel_id=1, source_target_pairs={{0,1},{1,0},{2,3},{3,2},{4,5},{5,4},{6,7},{7,6},{8,9},{9,8},{10,11... | collective-permute-start | bytes 1572872 | tf_op jit(solution)/shard_map/ppermute | solution.py:185
  101.5 48.2 %collective-permute-start.9 = (bf16[256,1024]{1,0:T(8,128)(2,1)S(1)}, bf16[256,1024]{1,0:T(8,128)(2,1)S(1)}, u32[]{:S(2)}, u32[]{:S(2)}) collective-permute-start(bf16[256,1024]{1,0:T(8,128)(2,1)S(1)} %get-tuple-element.34), channel_id=1, source_target_pairs={{0,2},{1,3},{2,0},{3,1},{4,6},{5,7},{6,4},{7,5},{8,10},{9,11},{10,... | collective-permute-start | bytes 1572872 | tf_op jit(solution)/shard_map/ppermute | solution.py:178
  105.7 23.0 %collective-permute-start.13 = (bf16[256,1024]{1,0:T(8,128)(2,1)S(1)}, bf16[256,1024]{1,0:T(8,128)(2,1)S(1)}, u32[]{:S(2)}, u32[]{:S(2)}) collective-permute-start(bf16[256,1024]{1,0:T(8,128)(2,1)S(1)} %collective-permute-done.11.k1.v1), channel_id=1, source_target_pairs={{0,1},{1,0},{2,3},{3,2},{4,5},{5,4},{6,7},{7,6},{8,9},{9,8},{10,11... | collective-permute-start | bytes 1572872 | tf_op jit(solution)/shard_map/ppermute | solution.py:186
  128.2 22.0 %collective-permute-start.14 = (bf16[256,1024]{1,0:T(8,128)(2,1)S(1)}, bf16[256,1024]{1,0:T(8,128)(2,1)S(1)}, u32[]{:S(2)}, u32[]{:S(2)}) collective-permute-start(bf16[256,1024]{1,0:T(8,128)(2,1)S(1)} %get-tuple-element.14), channel_id=1, source_target_pairs={{0,1},{1,0},{2,3},{3,2},{4,5},{5,4},{6,7},{7,6},{8,9},{9,8},{10,11... | collective-permute-start | bytes 1572872 | tf_op jit(solution)/shard_map/ppermute | solution.py:185
  128.2 22.0 %collective-permute-start.15 = (bf16[256,1024]{1,0:T(8,128)(2,1)S(1)}, bf16[256,1024]{1,0:T(8,128)(2,1)S(1)}, u32[]{:S(2)}, u32[]{:S(2)}) collective-permute-start(bf16[256,1024]{1,0:T(8,128)(2,1)S(1)} %collective-permute-done.1.k1.v1), channel_id=1, source_target_pairs={{0,1},{1,0},{2,3},{3,2},{4,5},{5,4},{6,7},{7,6},{8,9},{9,8},{10,11... | collective-permute-start | bytes 1572872 | tf_op jit(solution)/shard_map/ppermute | solution.py:186
  149.7 14.6 %collective-permute-start.16 = (bf16[256,1024]{1,0:T(8,128)(2,1)S(1)}, bf16[256,1024]{1,0:T(8,128)(2,1)S(1)}, u32[]{:S(2)}, u32[]{:S(2)}) collective-permute-start(bf16[256,1024]{1,0:T(8,128)(2,1)S(1)} %get-tuple-element.16), channel_id=1, source_target_pairs={{0,1},{1,0},{2,3},{3,2},{4,5},{5,4},{6,7},{7,6},{8,9},{9,8},{10,11... | collective-permute-start | bytes 1572872 | tf_op jit(solution)/shard_map/ppermute | solution.py:185
  149.7 14.6 %collective-permute-start.17 = (bf16[256,1024]{1,0:T(8,128)(2,1)S(1)}, bf16[256,1024]{1,0:T(8,128)(2,1)S(1)}, u32[]{:S(2)}, u32[]{:S(2)}) collective-permute-start(bf16[256,1024]{1,0:T(8,128)(2,1)S(1)} %collective-permute-done.9.k1.v1), channel_id=1, source_target_pairs={{0,1},{1,0},{2,3},{3,2},{4,5},{5,4},{6,7},{7,6},{8,9},{9,8},{10,11... | collective-permute-start | bytes 1572872 | tf_op jit(solution)/shard_map/ppermute | solution.py:186
  178.1 30.9 %copy-start.18 = (f32[2048]{0:T(1024)S(1)}, f32[2048]{0:T(1024)}, u32[]{:S(2)}) copy-start(f32[2048]{0:T(1024)} %param.18) | copy-start | bytes 24580
  208.0 1.0 copy-start.3
  232.2 12.3 %copy-start.19 = (pred[128,4]{0,1:T(4,128)(4,1)S(1)}, pred[128,4]{0,1:T(4,128)(4,1)}, u32[]{:S(2)}) copy-start(pred[128,4]{0,1:T(4,128)(4,1)} %get-tuple-element.19) | copy-start | bytes 1540
  232.2 12.5 %copy-start.15 = (s32[128,4]{0,1:T(4,128)S(1)}, s32[128,4]{0,1:T(4,128)}, u32[]{:S(2)}) copy-start(s32[128,4]{0,1:T(4,128)} %param.22) | copy-start | bytes 6148
  232.2 12.8 %copy-start.21 = (f32[128,4]{0,1:T(4,128)S(1)}, f32[128,4]{0,1:T(4,128)}, u32[]{:S(2)}) copy-start(f32[128,4]{0,1:T(4,128)} %param.23) | copy-start | bytes 6148
  232.2 12.9 %copy-start.20 = (pred[128,4]{0,1:T(4,128)(4,1)S(1)}, pred[128,4]{0,1:T(4,128)(4,1)}, u32[]{:S(2)}) copy-start(pred[128,4]{0,1:T(4,128)(4,1)} %get-tuple-element.17) | copy-start | bytes 1540
  232.2 13.0 %copy-start.17 = (s32[512]{0:T(512)S(1)}, s32[512]{0:T(512)}, u32[]{:S(2)}) copy-start(s32[512]{0:T(512)} %copy-done.16) | copy-start | bytes 6148
  240.3 18.6 %all-to-all-start.1 = ((bf16[16,2,4,2048]{3,2,1,0:T(4,128)(2,1)}), bf16[16,2,4,2048]{3,2,1,0:T(4,128)(2,1)S(1)}, u32[]{:S(2)}, u32[]{:S(2)}) async-start(bf16[16,2,4,2048]{3,2,1,0:T(4,128)(2,1)} %bitcast.12), calls=%async_computation.1 | async-start | bytes 1048576 | tf_op jit(solution)/shard_map/all_to_all | solution.py:275
  261.5 7.9 %copy-start.4 = (f32[128,2048]{1,0:T(8,128)S(1)}, f32[128,2048]{1,0:T(8,128)}, u32[]{:S(2)}) copy-start(f32[128,2048]{1,0:T(8,128)} %copy-done.3) | copy-start | bytes 3145732
Sparse Core Ops, SparseCore 0:
  9.5 190.2 all-gather.1
